TPU v7x, 32 devices: a whole 2x2x4 slice. The times are simulated.
32 devices in a mesh: replica: 2 (over y), fsdp: 16 (over z, x, core).
Axes of the slice: x: 2, y: 2, z: 4, core: 2. Of those that a mesh axis runs over, the one named last changes fastest.
Arguments:
- grads: bfloat16 [2, 2, 1024, 8192], P('replica', None, 'fsdp'), may hold values from -6 to 6
- errors: float32 [2, 2, 1024, 8192], P('replica', None, 'fsdp'), may hold values from -4 to 4
- basis: float32 [8192, 2, 32], P('fsdp'), may hold values from -6 to 6
Outputs:
- new_errors: float32 [2, 2, 1024, 8192], P('replica', None, 'fsdp')
- left_factor: float32 [2, 1024, 32], P(None, 'fsdp')
- new_basis: float32 [8192, 2, 32], P('fsdp')
All inputs are finite; a program needn't handle non-finite values.
Results may differ from a plain program's by a relative error of at most 0.0003.
Values sent between devices are 32-bit elements; how exact they have to be, the bound alone decides.
A program may use at most 64 MiB of HBM per device.

v0:
```python
import jax
import jax.numpy as jnp
from jax import lax
from jax.sharding import PartitionSpec as P


def shards(grads, errors, basis):
    highest = lax.Precision.HIGHEST
    merged = grads[0].astype(jnp.float32) + errors[0]
    replicas = lax.axis_size("replica")
    shard_cols = basis.shape[0]
    local_factor = jnp.einsum(
        "mrd,dmk->mrk", merged, lax.all_gather(basis, "fsdp", axis=0, tiled=True), precision=highest
    )
    factor = lax.psum(local_factor, "replica") / replicas
    local_gram = jnp.einsum("mrk,mrl->mkl", factor, factor, precision=highest)
    gram = lax.psum(local_gram, "fsdp")
    chol = jnp.linalg.cholesky(gram)

    def solve_one(lower, block):
        return jax.scipy.linalg.solve_triangular(lower, block.T, lower=True).T

    left_factor = jax.vmap(solve_one)(chol, factor)
    term = jnp.einsum("mrd,mrk->dmk", merged, left_factor, precision=highest)
    total = lax.psum(term, ("replica", "fsdp")) / replicas
    begin = lax.axis_index("fsdp") * shard_cols
    new_basis = lax.dynamic_slice_in_dim(total, begin, shard_cols, 0)
    approx = jnp.einsum("mrk,dmk->mrd", left_factor, total, precision=highest)
    new_errors = merged - approx
    return (new_errors[None], left_factor, new_basis)


def solution(mesh):
    in_specs = (
        P("replica", None, "fsdp", None),
        P("replica", None, "fsdp", None),
        P("fsdp", None, None),
    )
    out_specs = (P("replica", None, "fsdp", None), P(None, "fsdp", None), P("fsdp", None, None))
    return jax.shard_map(shards, mesh=mesh, in_specs=in_specs, out_specs=out_specs, check_vma=False)
```

profile of v0, /device:TPU:0, one launch (start us, length us, event | category | flops | bytes accessed | tf_op | source)
XLA Modules:
  0.0 292.6 jit_solution(15864588046567361826)
XLA Ops:
  7.2 0.0 all-gather.2.cloned.1.call-start
  7.2 0.7 all-gather.2.cloned.1.call-update
  7.9 0.0 all-reduce.2.cloned.1.call-start
  8.0 0.0 copy-start.1
  8.0 46.4 %all-gather.2.cloned.1.call-done = f32[8192,2,32]{0,2,1:T(8,128)} async-done(((f32[512,2,32]{0,2,1:T(8,128)}), f32[8192,2,32]{0,2,1:T(8,128)}) %all-gather.2.cloned.1.call-update) | async-done | bytes 2097168 | tf_op jit(solution)/shard_map/all_gather | solution.py:13
  54.4 7.3 %fusion.2 = f32[2,64,32]{1,2,0:T(8,128)S(1)} fusion(f32[8192,2,32]{0,2,1:T(8,128)} %all-gather.2.cloned.1.call-done, f32[1,2,64,8192]{3,2,1,0:T(8,128)} %param.4, bf16[1,2,64,8192]{3,2,1,0:T(8,128)(2,1)} %param.3), kind=kOutput, calls=%fused_computation.4 | convolution fusion | flops 404750336 | bytes 8404992 | tf_op jit(solution)/shard_map/mrd,dmk->mrk/dot_general | solution.py:12
  61.7 8.3 %psum.21 = f32[2,64,32]{1,2,0:T(8,128)S(1)} all-reduce(f32[2,64,32]{1,2,0:T(8,128)S(1)} %fusion.2), channel_id=1, replica_groups=mesh['replica'=2,'fsdp'=16] {'replica'}, use_global_device_ids=true, to_apply=%region_0.0 | all-reduce | flops 4096 | bytes 32768 | tf_op jit(solution)/shard_map/psum | solution.py:15
  70.0 0.2 fusion.8
  70.2 57.6 %psum.22 = f32[2,32,32]{1,2,0:T(8,128)S(1)} all-reduce(f32[2,32,32]{1,2,0:T(8,128)S(1)} %fusion.8), channel_id=1, replica_groups=mesh['replica'=2,'fsdp'=16] {'fsdp'}, use_global_device_ids=true, to_apply=%region_1.0 | all-reduce | flops 2048 | bytes 16384 | tf_op jit(solution)/shard_map/psum | solution.py:17
  127.9 0.1 copy.10
  127.9 5.9 %custom-call.8 = f32[2,32,32]{2,1,0:T(8,128)S(1)} custom-call(f32[2,32,32]{2,1,0:T(8,128)S(1)} %fusion.6), custom_call_target="Cholesky" | custom-call | tf_op jit(solution)/shard_map/jit(cholesky)/cholesky | solution.py:18
  133.8 0.1 compare_reduce_fusion
  134.0 0.1 select_bitcast_fusion
  134.0 4.9 %custom-call.9 = f32[2,1,32,32]{2,3,1,0:T(8,128)S(1)} custom-call(f32[2,1,32,32]{3,2,1,0:T(8,128)S(1)} %select_bitcast_fusion), custom_call_target="InvertDiagBlocksLowerTriangular" | custom-call | tf_op jit(solution)/shard_map/vmap(jit(_solve_triangular))/triangular_solve | solution.py:21
  139.0 0.2 fusion.4
  139.2 0.0 copy-done.1
  139.2 0.0 copy-start.2
  139.3 5.8 %convolution_bitcast_fusion = f32[8192,2,32]{0,2,1:T(8,128)} fusion(f32[2,32,64]{2,1,0:T(8,128)S(1)} %fusion.4, f32[1,2,64,8192]{3,2,1,0:T(8,128)} %param.4, bf16[1,2,64,8192]{3,2,1,0:T(8,128)(2,1)S(1)} %copy-done.1), kind=kOutput, calls=%fused_computation.2 | convolution fusion | flops 404750336 | bytes 8404992 | tf_op jit(solution)/shard_map/mrd,mrk->dmk/dot_general | solution.py:24
  145.1 0.0 all-reduce.2.cloned.1.call-update
  145.1 130.2 %all-reduce.2.cloned.1.call-done = f32[8192,2,32]{0,2,1:T(8,128)} async-done(((f32[8192,2,32]{0,2,1:T(8,128)}), f32[8192,2,32]{0,2,1:T(8,128)}) %all-reduce.2.cloned.1.call-update) | async-done | bytes 2097168 | tf_op jit(solution)/shard_map/psum | solution.py:25
  275.4 0.0 copy-start
  275.4 1.9 broadcast_multiply_fusion
  277.3 0.7 constant_dynamic-slice_fusion
  277.9 0.0 copy-done.2
  277.9 0.2 copy-done
  278.2 7.6 %fusion = f32[1,2,64,8192]{3,2,1,0:T(8,128)} fusion(f32[2,32,64]{2,1,0:T(8,128)S(1)} %fusion.4, f32[1,2,64,8192]{3,2,1,0:T(8,128)S(1)} %copy-done, bf16[1,2,64,8192]{3,2,1,0:T(8,128)(2,1)S(1)} %copy-done.1, f32[8192,2,32]{0,2,1:T(8,128)} %all-reduce.2.cloned.1.call-done), kind=kOutput, calls=%fused_computation.1 | convolution fusion | flops 406323200 | bytes 12599296 | tf_op jit(solution)/shard_map/mrk,dmk->mrd/dot_general | solution.py:28
  (4 shorter events, 0.1 us)
Async XLA Ops:
  7.2 47.2 %all-gather.2.cloned.1.call-start = ((), (), s32[]{:S(2)}) async-start(), calls=%async_computation | async-start | bytes 2228224 | tf_op jit(solution)/shard_map/all_gather | solution.py:13
  7.9 267.5 %all-reduce.2.cloned.1.call-start = ((), (), s32[]{:S(2)}) async-start(), calls=%async_computation.1 | async-start | bytes 4194304 | tf_op jit(solution)/shard_map/psum | solution.py:25
  8.0 131.3 %copy-start.1 = (bf16[1,2,64,8192]{3,2,1,0:T(8,128)(2,1)S(1)}, bf16[1,2,64,8192]{3,2,1,0:T(8,128)(2,1)}, u32[]{:S(2)}) copy-start(bf16[1,2,64,8192]{3,2,1,0:T(8,128)(2,1)} %param.3) | copy-start | bytes 6291460
  139.2 138.7 %copy-start.2 = (f32[2,32,64]{2,1,0:T(8,128)}, f32[2,32,64]{2,1,0:T(8,128)S(1)}, u32[]{:S(2)}) copy-start(f32[2,32,64]{2,1,0:T(8,128)S(1)} %fusion.4) | copy-start | bytes 49156
  275.4 2.8 copy-start
Sparse Core Ops, SparseCore 0:
  10.2 44.1 all-gather.1
  145.2 130.0 all-reduce.1
where the time goes:
time: 293 us
  waiting for transfers between devices  177 us (60%)
  blocking collectives  66 us (23%)
  matrix products  21.2 us (7%)
  between operations  14.1 us (5%)
  other arithmetic  13 us (4%)
    psum x1, waiting for transfers between devices, shards(): total = lax.psum(term, ('replica', 'fsdp')) / replicas  130 us
    psum x1, blocking collectives, shards(): gram = lax.psum(local_gram, 'fsdp')  57.6 us
    all_gather x1, waiting for transfers between devices, shards(): lax.all_gather(basis, 'fsdp', axis=0, tiled=True)  46.4 us
    psum x1, blocking collectives, shards(): factor = lax.psum(local_factor, 'replica') / replicas  8.33 us
    dot_general x1, matrix products, shards(): approx = jnp.einsum('mrk,dmk->mrd', left_factor, total, precision=highest)  7.6 us
    dot_general x1, matrix products, shards(): jnp.einsum('mrd,dmk->mrk', merged, lax.all_gather(basis, 'fsdp', axis=0,...  7.34 us
    another operation x4, other arithmetic, shards(): chol = jnp.linalg.cholesky(gram)  6.03 us
  transfers between devices with their start and end apart: 2, of which 2 were waited for; matrix products, arithmetic and copies ran while one was open for 0% of the time, Pallas kernels for 0%

commit v1 on v0

v1 whole, which is shorter than its diff:
```python
import functools

import jax
import jax.numpy as jnp
from jax import lax
from jax.experimental import pallas as pl
from jax.experimental.pallas import tpu as pltpu
from jax.sharding import PartitionSpec as P

MESH = pl.DeviceIdType.MESH
F32, BF16 = jnp.float32, jnp.bfloat16
TILE = 512
LANES = 128
NT = (((1,), (1,)), ((), ()))
NN = (((1,), (0,)), ((), ()))
TN = (((0,), (0,)), ((), ()))


def split(x):
    high = x.astype(BF16)
    return high, (x - high.astype(F32)).astype(BF16)


def dot32(a, b, dims):
    (ca,), (cb,) = dims[0]
    ah, al = split(a)
    bh, bl = split(b)
    left = jnp.concatenate([ah, ah, al], axis=ca)
    right = jnp.concatenate([bh, bl, bh], axis=cb)
    return lax.dot_general(left, right, dims, preferred_element_type=F32)


def log2(n):
    return n.bit_length() - 1


def orders(nb, nr):
    core = [("fsdp", 0)]
    near = [("fsdp", 1)]
    far = [("fsdp", b) for b in range(2, nb)]
    across = [("replica", b) for b in range(nr)]
    reduce_parts = [
        (0, 24, core + near + across + far),
        (24, 48, core + across + far + near),
        (48, 64, core + far + near + across),
    ]
    back = far[::-1]
    gather_parts = [back + near + core, near + back + core]
    return reduce_parts, gather_parts


def exchange(
    n, replicas, grads, errors, basis, total, left_t, own_basis, inverse,
    held, g_buf, e_buf, mhl, acc, ft, ft_in, z, z_in, gram, gram_in,
    load_sem, a_send, a_recv, f_send, f_recv, s_send, s_recv, m_send, m_recv, b_send, b_recv,
):
    nb, nr = log2(n), log2(replicas)
    reduce_parts, gather_parts = orders(nb, nr)
    rank = basis.shape[0] // 2
    width = basis.shape[1]
    rows = grads.shape[1]
    cols = grads.shape[2]
    y, f = lax.axis_index("replica"), lax.axis_index("fsdp")

    def bit_of(axis, bit):
        return lax.rem(lax.div(f if axis == "fsdp" else y, 1 << bit), 2)

    def partner(axis, bit):
        step = (1 - 2 * bit_of(axis, bit)) * (1 << bit)
        return (y, f + step) if axis == "fsdp" else (y + step, f)

    loads = [
        pltpu.make_async_copy(grads, g_buf, load_sem.at[0]),
        pltpu.make_async_copy(errors, e_buf, load_sem.at[1]),
    ]
    for load in loads:
        load.start()

    links = [("fsdp", b) for b in range(nb)] + [("replica", b) for b in range(nr)]
    barrier = pltpu.get_barrier_semaphore()
    for link in links:
        pl.semaphore_signal(barrier, inc=1, device_id=partner(*link), device_id_type=MESH)
    mine = tuple(bit_of("fsdp", b) for b in range(nb - 1, -1, -1))
    held[mine] = basis[...]
    pl.semaphore_wait(barrier, len(links))

    def gather_copy(part, step):
        done = [bit for _, bit in gather_parts[part][:step]]
        at = tuple(slice(None) if b in done else bit_of("fsdp", b) for b in range(nb - 1, -1, -1))
        at = at + (pl.ds(part * rank, rank), slice(None))
        return pltpu.make_async_remote_copy(
            src_ref=held.at[at], dst_ref=held.at[at],
            send_sem=a_send.at[part, step], recv_sem=a_recv.at[part, step],
            device_id=partner(*gather_parts[part][step]), device_id_type=MESH,
        )

    def factor_tile(part, shard):
        at = tuple(lax.rem(lax.div(shard, 1 << b), 2) for b in range(nb - 1, -1, -1))
        high, low = split(held[at + (pl.ds(part * rank, rank), slice(None))])
        here = pl.ds(pl.multiple_of(shard * width, width), width)
        acc[part] += lax.dot_general(
            jnp.concatenate([high, low], axis=0), mhl[part, :, here], NT, preferred_element_type=F32
        )

    def factor_step(part, step):
        done = [bit for _, bit in gather_parts[part][:step]]
        now = gather_parts[part][step][1]
        base = sum(
            ((1 - bit_of("fsdp", b)) if b == now else bit_of("fsdp", b)) * (1 << b)
            for b in range(nb) if b not in done
        )

        @pl.loop(0, 1 << step)
        def _(j):
            shard = base
            for i, b in enumerate(done):
                shard = shard + lax.rem(lax.div(j, 1 << i), 2) * (1 << b)
            factor_tile(part, shard)

    copies = [gather_copy(part, 0) for part in range(2)]
    for copy in copies:
        copy.start()
    acc[...] = jnp.zeros_like(acc)
    for load in loads:
        load.wait()

    @pl.loop(0, cols // TILE)
    def _(t):
        here = pl.ds(pl.multiple_of(t * TILE, TILE), TILE)
        for m in range(2):
            high, low = split(g_buf[m, :, here].astype(F32) + e_buf[m, :, here])
            mhl[m, 0:rows, here] = high
            mhl[m, rows : 2 * rows, here] = low

    for part in range(2):
        factor_tile(part, f)
    for step in range(nb):
        for copy in copies:
            copy.wait()
        if step + 1 < nb:
            copies = [gather_copy(part, step + 1) for part in range(2)]
            for copy in copies:
                copy.start()
        for part in range(2):
            factor_step(part, step)

    for m in range(2):
        whole = acc[m, 0:rank] + acc[m, rank : 2 * rank]
        one = whole[:, 0:rows] + whole[:, rows : 2 * rows]
        ft[0, m * rank : (m + 1) * rank] = jnp.concatenate([one, one], axis=1)
    for b in range(nr):
        copy = pltpu.make_async_remote_copy(
            src_ref=ft.at[b], dst_ref=ft_in.at[b], send_sem=f_send.at[b], recv_sem=f_recv.at[b],
            device_id=partner("replica", b), device_id_type=MESH,
        )
        copy.start()
        copy.wait()
        ft[b + 1] = ft[b] + ft_in[b]
    factor = ft[nr] * (1.0 / replicas)
    f_high, f_low = split(factor)
    weights = [
        jnp.concatenate([f_high[m * rank : (m + 1) * rank], f_low[m * rank : (m + 1) * rank]], axis=0)
        for m in range(2)
    ]

    def term(start, count):
        @pl.loop(0, count // TILE)
        def _(t):
            here = pl.ds(pl.multiple_of(start + t * TILE, TILE), TILE)
            for m in range(2):
                out = lax.dot_general(weights[m], mhl[m, :, here], NN, preferred_element_type=F32)
                z[m * rank : (m + 1) * rank, here] = out[0:rank] + out[rank : 2 * rank]

    nsteps = nb + nr
    half = cols // 2
    core = bit_of("fsdp", 0)
    term((1 - core) * half, half)
    starts = [0 for _ in reduce_parts]
    sizes = [cols for _ in reduce_parts]
    history = [[] for _ in reduce_parts]
    offset = 0
    for step in range(nsteps):
        pieces = []
        size = sizes[0]
        cut = size > LANES
        part_size = size // 2 if cut else size
        for p, (low, high, order) in enumerate(reduce_parts):
            link = order[step]
            bit = bit_of(*link)
            away = starts[p] + (1 - bit) * part_size if cut else starts[p]
            keep = starts[p] + bit * part_size if cut else starts[p]
            away = pl.multiple_of(away, LANES)
            copy = pltpu.make_async_remote_copy(
                src_ref=z.at[pl.ds(low, high - low), pl.ds(away, part_size)],
                dst_ref=z_in.at[pl.ds(low, high - low), pl.ds(offset, part_size)],
                send_sem=s_send.at[p, step], recv_sem=s_recv.at[p, step],
                device_id=partner(*link), device_id_type=MESH,
            )
            copy.start()
            history[p].append((link, bit, cut))
            pieces.append((copy, keep))
        if step == 0:
            term(core * half, half)
            product = lax.dot_general(
                factor, jnp.concatenate([factor, factor], axis=0), NT,
                precision=lax.Precision.HIGHEST, preferred_element_type=F32,
            ) * 0.5
            lane = lax.broadcasted_iota(jnp.int32, (rank, LANES), 1)
            gram[0] = jnp.where(lane < rank, product[0:rank], product[rank : 2 * rank])
        link = reduce_parts[0][2][step]
        g_copy = None
        if link[0] == "fsdp":
            g_copy = pltpu.make_async_remote_copy(
                src_ref=gram.at[step], dst_ref=gram_in.at[step],
                send_sem=m_send.at[step], recv_sem=m_recv.at[step],
                device_id=partner(*link), device_id_type=MESH,
            )
            g_copy.start()
        for p, (low, high, order) in enumerate(reduce_parts):
            copy, keep = pieces[p]
            copy.wait()
            here = pl.ds(pl.multiple_of(keep, LANES), part_size)
            z[low:high, here] = z[low:high, here] + z_in[low:high, offset : offset + part_size]
            starts[p], sizes[p] = keep, part_size
        if g_copy is not None:
            g_copy.wait()
            gram[step + 1] = gram[step] + gram_in[step]
        else:
            gram[step + 1] = gram[step]
        offset += part_size

    for p, (low, high, _) in enumerate(reduce_parts):
        here = pl.ds(pl.multiple_of(starts[p], LANES), sizes[p])
        total[low:high, here] = z[low:high, here]

    def back(step):
        out = []
        for p, (low, high, _) in enumerate(reduce_parts):
            link, bit, cut = history[p][step]
            if not cut:
                continue
            at = (pl.ds(low, high - low), pl.ds(pl.multiple_of(starts[p], LANES), sizes[p]))
            copy = pltpu.make_async_remote_copy(
                src_ref=total.at[at], dst_ref=total.at[at],
                send_sem=b_send.at[p, step], recv_sem=b_recv.at[p, step],
                device_id=partner(*link), device_id_type=MESH,
            )
            copy.start()
            out.append(copy)
            starts[p] = starts[p] - bit * sizes[p]
            sizes[p] = 2 * sizes[p]
        return out

    copies = back(nsteps - 1)

    row = lax.broadcasted_iota(jnp.int32, (rank, LANES), 0)
    lane = lax.broadcasted_iota(jnp.int32, (rank, LANES), 1)
    first = lax.rem(lane, 2 * rank) < rank
    work = jnp.where(lane < 2 * rank, gram[nsteps], jnp.where(lax.rem(lane, rank) == row, 1.0, 0.0))
    for j in range(rank):
        column = jnp.where(first, work[:, j : j + 1], work[:, rank + j : rank + j + 1])
        top = work[j : j + 1, :] / column[j : j + 1, :]
        work = jnp.where(row > j, work - column * top, work)
    pivots = [
        jnp.sum(jnp.where(lane == row + m * rank, work, 0.0), axis=1, keepdims=True) for m in range(2)
    ]
    scaled = work / jnp.sqrt(jnp.where(first, pivots[0], pivots[1]))
    inv = [scaled[:, (2 + m) * rank : (3 + m) * rank] for m in range(2)]
    for m in range(2):
        inverse[m * rank : (m + 1) * rank] = inv[m]
        left_t[m * rank : (m + 1) * rank] = lax.dot_general(
            inv[m], factor[m * rank : (m + 1) * rank, 0:rows], NN,
            precision=lax.Precision.HIGHEST, preferred_element_type=F32,
        )

    for step in range(nsteps - 1, -1, -1):
        for copy in copies:
            copy.wait()
        if step > 0:
            copies = back(step - 1)
    own = pl.ds(pl.multiple_of(f * width, LANES), width)
    for m in range(2):
        at = slice(m * rank, (m + 1) * rank)
        own_basis[at] = dot32(inv[m], total[at, own], NN) * (1.0 / replicas)


def finish(replicas, grads, errors, total, left_t, inverse, out):
    rank = total.shape[0] // 2
    for m in range(2):
        at = slice(m * rank, (m + 1) * rank)
        basis = dot32(inverse[at], total[at], NN) * (1.0 / replicas)
        approx = dot32(left_t[at], basis, TN)
        out[m] = grads[m].astype(F32) + errors[m] - approx


def solution(mesh):
    n, replicas = mesh.shape["fsdp"], mesh.shape["replica"]
    nb, nr = log2(n), log2(replicas)
    steps = nb + nr

    def shards(grads, errors, basis):
        _, nmat, rows, cols = grads.shape
        width, _, rank = basis.shape
        grads, errors = grads[0], errors[0]
        basis_t = jnp.transpose(basis, (1, 2, 0)).reshape(nmat * rank, width)
        full = nmat * rank
        vmem = pl.BlockSpec(memory_space=pltpu.VMEM)
        hbm = pl.BlockSpec(memory_space=pl.ANY)
        dma = pltpu.SemaphoreType.DMA
        total, left_t, own_basis, inverse = pl.pallas_call(
            functools.partial(exchange, n, replicas),
            out_shape=[
                jax.ShapeDtypeStruct((full, cols), F32),
                jax.ShapeDtypeStruct((full, rows), F32),
                jax.ShapeDtypeStruct((full, width), F32),
                jax.ShapeDtypeStruct((full, rank), F32),
            ],
            in_specs=[hbm, hbm, vmem],
            out_specs=[vmem] * 4,
            scratch_shapes=[
                pltpu.VMEM((2,) * nb + (full, width), F32),
                pltpu.VMEM((nmat, rows, cols), BF16),
                pltpu.VMEM((nmat, rows, cols), F32),
                pltpu.VMEM((nmat, 2 * rows, cols), BF16),
                pltpu.VMEM((nmat, 2 * rank, 2 * rows), F32),
                pltpu.VMEM((nr + 1, full, 2 * rows), F32),
                pltpu.VMEM((nr, full, 2 * rows), F32),
                pltpu.VMEM((full, cols), F32),
                pltpu.VMEM((full, cols + LANES * steps), F32),
                pltpu.VMEM((steps + 1, rank, LANES), F32),
                pltpu.VMEM((steps, rank, LANES), F32),
                dma((2,)),
                dma((2, nb)), dma((2, nb)),
                dma((nr,)), dma((nr,)),
                dma((3, steps)), dma((3, steps)),
                dma((steps,)), dma((steps,)),
                dma((3, steps)), dma((3, steps)),
            ],
            compiler_params=pltpu.CompilerParams(
                collective_id=0, has_side_effects=True, vmem_limit_bytes=40 * 1024 * 1024
            ),
        )(grads, errors, basis_t)

        block = 1024
        whole = lambda a: pl.BlockSpec(a.shape, lambda i: (0, 0))
        new_errors = pl.pallas_call(
            functools.partial(finish, replicas),
            grid=(cols // block,),
            out_shape=jax.ShapeDtypeStruct((nmat, rows, cols), F32),
            in_specs=[
                pl.BlockSpec((nmat, rows, block), lambda i: (0, 0, i)),
                pl.BlockSpec((nmat, rows, block), lambda i: (0, 0, i)),
                pl.BlockSpec((full, block), lambda i: (0, i)),
                whole(left_t),
                whole(inverse),
            ],
            out_specs=pl.BlockSpec((nmat, rows, block), lambda i: (0, 0, i)),
            compiler_params=pltpu.CompilerParams(vmem_limit_bytes=32 * 1024 * 1024),
        )(grads, errors, total, left_t, inverse)
        left = jnp.transpose(left_t.reshape(nmat, rank, rows), (0, 2, 1))
        new_basis = jnp.transpose(own_basis.reshape(nmat, rank, width), (2, 0, 1))
        return (new_errors[None], left, new_basis)

    in_specs = (
        P("replica", None, "fsdp", None),
        P("replica", None, "fsdp", None),
        P("fsdp", None, None),
    )
    out_specs = (P("replica", None, "fsdp", None), P(None, "fsdp", None), P("fsdp", None, None))
    return jax.shard_map(shards, mesh=mesh, in_specs=in_specs, out_specs=out_specs, check_vma=False)
```

time: 293 us -> 91.3 us (0.31)
  waiting for transfers between devices: 177 us -> 0 us
  Pallas kernels: 0 us -> 84.5 us
  blocking collectives: 66 us -> 0 us
  matrix products: 21.2 us -> 0 us
  between operations: 14.1 us -> 0.66 us
  other arithmetic: 13 us -> 0 us
  local copies, waits for them, and re-layouts: 0.99 us -> 5.95 us
    psum x1 -> x0, waiting for transfers between devices: 130 us -> none  [shards(): total = lax.psum(term, ('replica', 'fsdp')) / replicas]
    pallas_call x0 -> x2, Pallas kernels: none -> 84.5 us  [the longest x1 78.1 us: shards(): pl.pallas_call(functools.partial(exchange, n, replicas), out_shape=[jax.S...]
    psum x2 -> x0, blocking collectives: 66 us -> none  [the longest x1 57.6 us: shards(): gram = lax.psum(local_gram, 'fsdp')]
    all_gather x1 -> x0, waiting for transfers between devices: 46.4 us -> none  [shards(): lax.all_gather(basis, 'fsdp', axis=0, tiled=True)]
    dot_general x4 -> x0, matrix products: 20.9 us -> none  [the longest x1 7.6 us: shards(): approx = jnp.einsum('mrk,dmk->mrd', left_factor, total, precision=highest)]
    another operation x7 -> x0, other arithmetic: 11.1 us -> none  [the longest x4 6.03 us: shards(): chol = jnp.linalg.cholesky(gram)]
    unnamed x6 -> x10, local copies, waits for them, and re-layouts: 0.24 us -> 5.95 us
  transfers between devices with their start and end apart: 2 -> 0, of which waited for: 2 -> 0; matrix products, arithmetic and copies ran while one was open for 0% -> 0% of each run, Pallas kernels for 0% -> 0%
where the time goes in v1:
time: 91.3 us; the launch traced here: 91.1 us
  Pallas kernels  84.5 us (93%)
  local copies, waits for them, and re-layouts  5.95 us (7%)
    pallas_call x1, Pallas kernels, shards(): pl.pallas_call(functools.partial(exchange, n, replicas), out_shape=[jax.S...  78.1 us
    pallas_call x1, Pallas kernels, shards(): pl.pallas_call(functools.partial(finish, replicas), grid=(cols // block,)...  6.35 us
    unnamed x10, local copies, waits for them, and re-layouts  5.95 us

profile of v1, /device:TPU:0, one launch (start us, length us, event | category | flops | bytes accessed | tf_op | source)
XLA Modules:
  0.0 91.1 jit_solution(3372492623332222140)
XLA Ops:
  0.6 0.0 copy-start
  0.6 2.2 %copy-done = f32[1,2,64,8192]{3,2,1,0:T(8,128)S(1)} copy-done((f32[1,2,64,8192]{3,2,1,0:T(8,128)S(1)}, f32[1,2,64,8192]{3,2,1,0:T(8,128)}, u32[]{:S(2)}) %copy-start) | copy-done | bytes 4194328
  2.8 0.0 copy-start.1
  2.8 1.6 %copy-done.1 = bf16[1,2,64,8192]{3,2,1,0:T(8,128)(2,1)S(1)} copy-done((bf16[1,2,64,8192]{3,2,1,0:T(8,128)(2,1)S(1)}, bf16[1,2,64,8192]{3,2,1,0:T(8,128)(2,1)}, u32[]{:S(2)}) %copy-start.1) | copy-done | bytes 2097176
  4.4 0.0 copy-start.3
  4.4 0.9 copy-done.3
  5.3 0.0 copy-start.2
  5.3 78.1 %shard_map.58 = (f32[64,8192]{1,0:T(8,128)S(1)}, f32[64,64]{1,0:T(8,128)S(1)}, f32[64,512]{1,0:T(8,128)S(1)}, f32[64,32]{1,0:T(8,128)S(1)}) custom-call(bf16[2,64,8192]{2,1,0:T(8,128)(2,1)S(1)} %bitcast.14, f32[2,64,8192]{2,1,0:T(8,128)S(1)} %bitcast.12, f32[64,512]{1,0:T(8,128)S(1)} %bitcast.17), custom_call_target="tpu_custom_call" | custom-call | tf_op jit(solution)/shard_map/pallas_call | solution.py:310
  83.5 0.0 copy-done.2
  83.5 6.4 %shard_map.59 = f32[2,64,8192]{2,1,0:T(8,128)} custom-call(bf16[2,64,8192]{2,1,0:T(8,128)(2,1)S(1)} %bitcast.15, f32[2,64,8192]{2,1,0:T(8,128)S(1)} %bitcast.13, f32[64,8192]{1,0:T(8,128)S(1)} %get-tuple-element.7.total, f32[64,64]{1,0:T(8,128)S(1)} %get-tuple-element.8.left_t, f32[64,32]{1,0:T(8,128)S(1)} %get-tuple-element.9.inverse), custom_call_target="tpu_custom_call" | custom-call | tf_op jit(solution)/shard_map/pallas_call | solution.py:346
  89.8 0.6 copy.8
  90.4 0.7 copy.9
Async XLA Ops:
  0.6 2.2 %copy-start = (f32[1,2,64,8192]{3,2,1,0:T(8,128)S(1)}, f32[1,2,64,8192]{3,2,1,0:T(8,128)}, u32[]{:S(2)}) copy-start(f32[1,2,64,8192]{3,2,1,0:T(8,128)} %param.4) | copy-start | bytes 12582916
  2.8 1.6 %copy-start.1 = (bf16[1,2,64,8192]{3,2,1,0:T(8,128)(2,1)S(1)}, bf16[1,2,64,8192]{3,2,1,0:T(8,128)(2,1)}, u32[]{:S(2)}) copy-start(bf16[1,2,64,8192]{3,2,1,0:T(8,128)(2,1)} %param.3) | copy-start | bytes 6291460
  4.4 0.9 copy-start.3
  5.3 78.2 %copy-start.2 = (bf16[1,2,64,8192]{3,2,1,0:T(8,128)(2,1)S(1)}, bf16[1,2,64,8192]{3,2,1,0:T(8,128)(2,1)}, u32[]{:S(2)}) copy-start(bf16[1,2,64,8192]{3,2,1,0:T(8,128)(2,1)} %param.3) | copy-start | bytes 6291460

commit v2 on v1

--- a/solution.py
+++ b/solution.py
@@ -39,10 +39,12 @@
     near = [("fsdp", 1)]
     far = [("fsdp", b) for b in range(2, nb)]
     across = [("replica", b) for b in range(nr)]
+    first = core + near + across + far
+    second = core + across + far + near
+    third = core + far + near + across
     reduce_parts = [
-        (0, 24, core + near + across + far),
-        (24, 48, core + across + far + near),
-        (48, 64, core + far + near + across),
+        (0, 8, first), (8, 24, first), (24, 32, third),
+        (32, 40, third), (40, 48, second), (48, 64, second),
     ]
     back = far[::-1]
     gather_parts = [back + near + core, near + back + core]
@@ -50,7 +52,7 @@
 
 
 def exchange(
-    n, replicas, grads, errors, basis, total, left_t, own_basis, inverse,
+    n, replicas, grads, errors, basis, total, left_t, own_basis, folded,
     held, g_buf, e_buf, mhl, acc, ft, ft_in, z, z_in, gram, gram_in,
     load_sem, a_send, a_recv, f_send, f_recv, s_send, s_recv, m_send, m_recv, b_send, b_recv,
 ):
@@ -135,12 +137,11 @@
     for part in range(2):
         factor_tile(part, f)
     for step in range(nb):
-        for copy in copies:
-            copy.wait()
-        if step + 1 < nb:
-            copies = [gather_copy(part, step + 1) for part in range(2)]
-            for copy in copies:
-                copy.start()
+        for part in range(2):
+            copies[part].wait()
+            if step + 1 < nb:
+                copies[part] = gather_copy(part, step + 1)
+                copies[part].start()
         for part in range(2):
             factor_step(part, step)
 
@@ -163,95 +164,96 @@
         for m in range(2)
     ]
 
-    def term(start, count):
+    def term(m, start, count):
         @pl.loop(0, count // TILE)
         def _(t):
             here = pl.ds(pl.multiple_of(start + t * TILE, TILE), TILE)
-            for m in range(2):
-                out = lax.dot_general(weights[m], mhl[m, :, here], NN, preferred_element_type=F32)
-                z[m * rank : (m + 1) * rank, here] = out[0:rank] + out[rank : 2 * rank]
+            out = lax.dot_general(weights[m], mhl[m, :, here], NN, preferred_element_type=F32)
+            z[m * rank : (m + 1) * rank, here] = out[0:rank] + out[rank : 2 * rank]
 
     nsteps = nb + nr
     half = cols // 2
     core = bit_of("fsdp", 0)
-    term((1 - core) * half, half)
-    starts = [0 for _ in reduce_parts]
-    sizes = [cols for _ in reduce_parts]
-    history = [[] for _ in reduce_parts]
-    offset = 0
+    parts = range(len(reduce_parts))
+    cuts, sizes, offsets = [], [cols], [0]
     for step in range(nsteps):
-        pieces = []
-        size = sizes[0]
-        cut = size > LANES
-        part_size = size // 2 if cut else size
-        for p, (low, high, order) in enumerate(reduce_parts):
-            link = order[step]
-            bit = bit_of(*link)
-            away = starts[p] + (1 - bit) * part_size if cut else starts[p]
-            keep = starts[p] + bit * part_size if cut else starts[p]
-            away = pl.multiple_of(away, LANES)
-            copy = pltpu.make_async_remote_copy(
-                src_ref=z.at[pl.ds(low, high - low), pl.ds(away, part_size)],
-                dst_ref=z_in.at[pl.ds(low, high - low), pl.ds(offset, part_size)],
-                send_sem=s_send.at[p, step], recv_sem=s_recv.at[p, step],
-                device_id=partner(*link), device_id_type=MESH,
-            )
-            copy.start()
-            history[p].append((link, bit, cut))
-            pieces.append((copy, keep))
-        if step == 0:
-            term(core * half, half)
-            product = lax.dot_general(
-                factor, jnp.concatenate([factor, factor], axis=0), NT,
-                precision=lax.Precision.HIGHEST, preferred_element_type=F32,
-            ) * 0.5
-            lane = lax.broadcasted_iota(jnp.int32, (rank, LANES), 1)
-            gram[0] = jnp.where(lane < rank, product[0:rank], product[rank : 2 * rank])
+        cuts.append(sizes[-1] > LANES)
+        sizes.append(sizes[-1] // 2 if cuts[-1] else sizes[-1])
+        offsets.append(offsets[-1] + sizes[-1])
+    starts = [[0] for _ in parts]
+
+    def send(p, step):
+        low, high, order = reduce_parts[p]
+        bit, size, start = bit_of(*order[step]), sizes[step + 1], starts[p][step]
+        away = start + (1 - bit) * size if cuts[step] else start
+        starts[p].append(start + bit * size if cuts[step] else start)
+        copy = pltpu.make_async_remote_copy(
+            src_ref=z.at[pl.ds(low, high - low), pl.ds(pl.multiple_of(away, LANES), size)],
+            dst_ref=z_in.at[pl.ds(low, high - low), pl.ds(offsets[step], size)],
+            send_sem=s_send.at[p, step], recv_sem=s_recv.at[p, step],
+            device_id=partner(*order[step]), device_id_type=MESH,
+        )
+        copy.start()
+        return copy
+
+    def gram_copy(step):
         link = reduce_parts[0][2][step]
-        g_copy = None
-        if link[0] == "fsdp":
-            g_copy = pltpu.make_async_remote_copy(
-                src_ref=gram.at[step], dst_ref=gram_in.at[step],
-                send_sem=m_send.at[step], recv_sem=m_recv.at[step],
-                device_id=partner(*link), device_id_type=MESH,
-            )
-            g_copy.start()
-        for p, (low, high, order) in enumerate(reduce_parts):
-            copy, keep = pieces[p]
-            copy.wait()
-            here = pl.ds(pl.multiple_of(keep, LANES), part_size)
-            z[low:high, here] = z[low:high, here] + z_in[low:high, offset : offset + part_size]
-            starts[p], sizes[p] = keep, part_size
+        if link[0] != "fsdp":
+            return None
+        copy = pltpu.make_async_remote_copy(
+            src_ref=gram.at[step], dst_ref=gram_in.at[step],
+            send_sem=m_send.at[step], recv_sem=m_recv.at[step],
+            device_id=partner(*link), device_id_type=MESH,
+        )
+        copy.start()
+        return copy
+
+    copies = []
+    for m in range(2):
+        term(m, (1 - core) * half, half)
+        copies += [send(p, 0) for p in parts if reduce_parts[p][0] // rank == m]
+    product = lax.dot_general(
+        factor, jnp.concatenate([factor, factor], axis=0), NT,
+        precision=lax.Precision.HIGHEST, preferred_element_type=F32,
+    ) * 0.5
+    lane = lax.broadcasted_iota(jnp.int32, (rank, LANES), 1)
+    gram[0] = jnp.where(lane < rank, product[0:rank], product[rank : 2 * rank])
+    g_copy = gram_copy(0)
+    for m in range(2):
+        term(m, core * half, half)
+    for step in range(nsteps):
+        size, offset = sizes[step + 1], offsets[step]
+        for p in parts:
+            low, high, _ = reduce_parts[p]
+            copies[p].wait()
+            here = pl.ds(pl.multiple_of(starts[p][step + 1], LANES), size)
+            added = z[low:high, here] + z_in[low:high, offset : offset + size]
+            if step + 1 < nsteps:
+                z[low:high, here] = added
+                copies[p] = send(p, step + 1)
+            else:
+                total[low:high, here] = added
         if g_copy is not None:
             g_copy.wait()
             gram[step + 1] = gram[step] + gram_in[step]
         else:
             gram[step + 1] = gram[step]
-        offset += part_size
-
-    for p, (low, high, _) in enumerate(reduce_parts):
-        here = pl.ds(pl.multiple_of(starts[p], LANES), sizes[p])
-        total[low:high, here] = z[low:high, here]
-
-    def back(step):
-        out = []
-        for p, (low, high, _) in enumerate(reduce_parts):
-            link, bit, cut = history[p][step]
-            if not cut:
-                continue
-            at = (pl.ds(low, high - low), pl.ds(pl.multiple_of(starts[p], LANES), sizes[p]))
-            copy = pltpu.make_async_remote_copy(
-                src_ref=total.at[at], dst_ref=total.at[at],
-                send_sem=b_send.at[p, step], recv_sem=b_recv.at[p, step],
-                device_id=partner(*link), device_id_type=MESH,
-            )
-            copy.start()
-            out.append(copy)
-            starts[p] = starts[p] - bit * sizes[p]
-            sizes[p] = 2 * sizes[p]
-        return out
-
-    copies = back(nsteps - 1)
+        g_copy = gram_copy(step + 1) if step + 1 < nsteps else None
+
+    def back(p, step):
+        low, high, order = reduce_parts[p]
+        if not cuts[step]:
+            return None
+        at = (pl.ds(low, high - low), pl.ds(pl.multiple_of(starts[p][step + 1], LANES), sizes[step + 1]))
+        copy = pltpu.make_async_remote_copy(
+            src_ref=total.at[at], dst_ref=total.at[at],
+            send_sem=b_send.at[p, step], recv_sem=b_recv.at[p, step],
+            device_id=partner(*order[step]), device_id_type=MESH,
+        )
+        copy.start()
+        return copy
+
+    copies = [back(p, nsteps - 1) for p in parts]
 
     row = lax.broadcasted_iota(jnp.int32, (rank, LANES), 0)
     lane = lax.broadcasted_iota(jnp.int32, (rank, LANES), 1)
@@ -267,30 +269,32 @@
     scaled = work / jnp.sqrt(jnp.where(first, pivots[0], pivots[1]))
     inv = [scaled[:, (2 + m) * rank : (3 + m) * rank] for m in range(2)]
     for m in range(2):
-        inverse[m * rank : (m + 1) * rank] = inv[m]
-        left_t[m * rank : (m + 1) * rank] = lax.dot_general(
+        solved = lax.dot_general(
             inv[m], factor[m * rank : (m + 1) * rank, 0:rows], NN,
             precision=lax.Precision.HIGHEST, preferred_element_type=F32,
         )
+        left_t[m * rank : (m + 1) * rank] = solved
+        folded[m * rank : (m + 1) * rank] = lax.dot_general(
+            inv[m], solved, TN, precision=lax.Precision.HIGHEST, preferred_element_type=F32
+        ) * (1.0 / replicas)
 
     for step in range(nsteps - 1, -1, -1):
-        for copy in copies:
-            copy.wait()
-        if step > 0:
-            copies = back(step - 1)
+        for p in parts:
+            if copies[p] is not None:
+                copies[p].wait()
+            if step > 0:
+                copies[p] = back(p, step - 1)
     own = pl.ds(pl.multiple_of(f * width, LANES), width)
     for m in range(2):
         at = slice(m * rank, (m + 1) * rank)
         own_basis[at] = dot32(inv[m], total[at, own], NN) * (1.0 / replicas)
 
 
-def finish(replicas, grads, errors, total, left_t, inverse, out):
+def finish(grads, errors, total, folded, out):
     rank = total.shape[0] // 2
     for m in range(2):
         at = slice(m * rank, (m + 1) * rank)
-        basis = dot32(inverse[at], total[at], NN) * (1.0 / replicas)
-        approx = dot32(left_t[at], basis, TN)
-        out[m] = grads[m].astype(F32) + errors[m] - approx
+        out[m] = grads[m].astype(F32) + errors[m] - dot32(folded[at], total[at], TN)
 
 
 def solution(mesh):
@@ -307,13 +311,13 @@
         vmem = pl.BlockSpec(memory_space=pltpu.VMEM)
         hbm = pl.BlockSpec(memory_space=pl.ANY)
         dma = pltpu.SemaphoreType.DMA
-        total, left_t, own_basis, inverse = pl.pallas_call(
+        total, left_t, own_basis, folded = pl.pallas_call(
             functools.partial(exchange, n, replicas),
             out_shape=[
                 jax.ShapeDtypeStruct((full, cols), F32),
                 jax.ShapeDtypeStruct((full, rows), F32),
                 jax.ShapeDtypeStruct((full, width), F32),
-                jax.ShapeDtypeStruct((full, rank), F32),
+                jax.ShapeDtypeStruct((full, rows), F32),
             ],
             in_specs=[hbm, hbm, vmem],
             out_specs=[vmem] * 4,
@@ -332,31 +336,30 @@
                 dma((2,)),
                 dma((2, nb)), dma((2, nb)),
                 dma((nr,)), dma((nr,)),
-                dma((3, steps)), dma((3, steps)),
+                dma((6, steps)), dma((6, steps)),
                 dma((steps,)), dma((steps,)),
-                dma((3, steps)), dma((3, steps)),
+                dma((6, steps)), dma((6, steps)),
             ],
             compiler_params=pltpu.CompilerParams(
-                collective_id=0, has_side_effects=True, vmem_limit_bytes=40 * 1024 * 1024
+                collective_id=0, has_side_effects=True, vmem_limit_bytes=60 * 1024 * 1024
             ),
         )(grads, errors, basis_t)
 
         block = 1024
         whole = lambda a: pl.BlockSpec(a.shape, lambda i: (0, 0))
         new_errors = pl.pallas_call(
-            functools.partial(finish, replicas),
+            finish,
             grid=(cols // block,),
             out_shape=jax.ShapeDtypeStruct((nmat, rows, cols), F32),
             in_specs=[
                 pl.BlockSpec((nmat, rows, block), lambda i: (0, 0, i)),
                 pl.BlockSpec((nmat, rows, block), lambda i: (0, 0, i)),
                 pl.BlockSpec((full, block), lambda i: (0, i)),
-                whole(left_t),
-                whole(inverse),
+                whole(folded),
             ],
             out_specs=pl.BlockSpec((nmat, rows, block), lambda i: (0, 0, i)),
-            compiler_params=pltpu.CompilerParams(vmem_limit_bytes=32 * 1024 * 1024),
-        )(grads, errors, total, left_t, inverse)
+            compiler_params=pltpu.CompilerParams(vmem_limit_bytes=60 * 1024 * 1024),
+        )(grads, errors, total, folded)
         left = jnp.transpose(left_t.reshape(nmat, rank, rows), (0, 2, 1))
         new_basis = jnp.transpose(own_basis.reshape(nmat, rank, width), (2, 0, 1))
         return (new_errors[None], left, new_basis)

time: 91.3 us -> 85.7 us (0.939)
  local copies, waits for them, and re-layouts: 5.95 us -> 1.28 us
  Pallas kernels: 84.5 us -> 83.4 us
    unnamed x10 -> x6, local copies, waits for them, and re-layouts: 5.95 us -> 1.28 us
    pallas_call x1, Pallas kernels: 78.1 us -> 75.1 us  [shards(): pl.pallas_call(functools.partial(exchange, n, replicas), out_shape=[jax.S...]
    pallas_call x1, Pallas kernels: 6.35 us -> 8.32 us  [shards(): pl.pallas_call(finish, grid=(cols // block,), out_shape=jax.ShapeDtypeStr...]
where the time goes in v2:
time: 85.7 us; the launch traced here: 85.4 us
  Pallas kernels  83.4 us (97%)
  local copies, waits for them, and re-layouts  1.28 us (1%)
    pallas_call x1, Pallas kernels, shards(): pl.pallas_call(functools.partial(exchange, n, replicas), out_shape=[jax.S...  75.1 us
    pallas_call x1, Pallas kernels, shards(): pl.pallas_call(finish, grid=(cols // block,), out_shape=jax.ShapeDtypeStr...  8.32 us

profile of v2, /device:TPU:0, one launch (start us, length us, event | category | flops | bytes accessed | tf_op | source)
XLA Modules:
  0.0 85.4 jit_solution(8920169808000001627)
XLA Ops:
  0.6 75.1 %shard_map.58 = (f32[64,8192]{1,0:T(8,128)}, f32[64,64]{1,0:T(8,128)}, f32[64,512]{1,0:T(8,128)}, f32[64,64]{1,0:T(8,128)}) custom-call(bf16[2,64,8192]{2,1,0:T(8,128)(2,1)} %bitcast.14, f32[2,64,8192]{2,1,0:T(8,128)} %bitcast.12, f32[64,512]{1,0:T(8,128)} %bitcast.17), custom_call_target="tpu_custom_call" | custom-call | tf_op jit(solution)/shard_map/pallas_call | solution.py:314
  75.8 0.0 copy-start.1
  75.8 0.0 copy-start
  75.8 8.3 %shard_map.59 = f32[2,64,8192]{2,1,0:T(8,128)} custom-call(bf16[2,64,8192]{2,1,0:T(8,128)(2,1)} %bitcast.15, f32[2,64,8192]{2,1,0:T(8,128)} %bitcast.13, f32[64,8192]{1,0:T(8,128)} %get-tuple-element.7.total, f32[64,64]{1,0:T(8,128)} %get-tuple-element.8.folded), custom_call_target="tpu_custom_call" | custom-call | tf_op jit(solution)/shard_map/pallas_call | solution.py:350
  84.1 0.0 copy-done.1
  84.1 0.6 copy.8
  84.7 0.0 copy-done
  84.7 0.7 copy.9
Async XLA Ops:
  75.8 8.3 %copy-start.1 = (f32[64,64]{1,0:T(8,128)S(1)}, f32[64,64]{1,0:T(8,128)}, u32[]{:S(2)}) copy-start(f32[64,64]{1,0:T(8,128)} %get-tuple-element.9) | copy-start | bytes 49156
  75.8 8.9 %copy-start = (f32[64,512]{1,0:T(8,128)S(1)}, f32[64,512]{1,0:T(8,128)}, u32[]{:S(2)}) copy-start(f32[64,512]{1,0:T(8,128)} %get-tuple-element.10) | copy-start | bytes 393220

commit v3 on v2

v3 whole, which is shorter than its diff:
```python
import functools

import jax
import jax.numpy as jnp
from jax import lax
from jax.experimental import pallas as pl
from jax.experimental.pallas import tpu as pltpu
from jax.sharding import PartitionSpec as P

MESH = pl.DeviceIdType.MESH
F32, BF16 = jnp.float32, jnp.bfloat16
TILE = 512
LANES = 128
NT = (((1,), (1,)), ((), ()))
NN = (((1,), (0,)), ((), ()))
TN = (((0,), (0,)), ((), ()))


def split(x):
    high = x.astype(BF16)
    return high, (x - high.astype(F32)).astype(BF16)


def dot32(a, b, dims):
    (ca,), (cb,) = dims[0]
    ah, al = split(a)
    bh, bl = split(b)
    left = jnp.concatenate([ah, ah, al], axis=ca)
    right = jnp.concatenate([bh, bl, bh], axis=cb)
    return lax.dot_general(left, right, dims, preferred_element_type=F32)


def log2(n):
    return n.bit_length() - 1


def plan(nb, nr, share):
    core, near = [("fsdp", 0)], [("fsdp", 1)]
    far = [("fsdp", b) for b in range(2, nb)]
    across = [("replica", b) for b in range(nr)]
    plane_first = [core, near + across, far]
    far_first = [core, far, near + across]
    reduce_parts = [
        (0, 16, plane_first), (16, 32, plane_first), (32, 40, plane_first),
        (40, 48, far_first), (48, 64, far_first),
    ]
    plane = near + across if share else near
    gather_parts = [(0, 40, [far, plane, core]), (40, 64, [plane, far, core])]
    return reduce_parts, gather_parts


def layout(nb, nr, cols):
    out = []
    for _, _, stages in plan(nb, nr, False)[0]:
        cuts, sizes, offsets = [], [cols], [0]
        for stage in stages:
            members = 1 << len(stage)
            cuts.append(sizes[-1] // members >= LANES)
            sizes.append(sizes[-1] // members if cuts[-1] else sizes[-1])
            offsets.append(offsets[-1] + (members - cuts[-1]) * sizes[-1])
        out.append((cuts, sizes, offsets))
    return out


def exchange(
    n, replicas, share, grads, errors, basis, total, left_t, own_basis, folded,
    held, g_buf, e_buf, mhl, acc, ft, ft_in, z, z_in, gram, gram_in,
    load_sem, a_send, a_recv, f_send, f_recv, s_send, s_recv, m_send, m_recv, b_send, b_recv,
):
    nb, nr = log2(n), log2(replicas)
    reduce_parts, gather_parts = plan(nb, nr, share)
    rank = basis.shape[0] // 2
    width = basis.shape[1]
    rows = grads.shape[1]
    cols = grads.shape[2]
    y, f = lax.axis_index("replica"), lax.axis_index("fsdp")

    def bit_of(link):
        return lax.rem(lax.div(f if link[0] == "fsdp" else y, 1 << link[1]), 2)

    def index_of(stage, mask=0):
        total_index = 0
        for i, link in enumerate(stage):
            own = bit_of(link)
            total_index = total_index + (1 - own if mask >> i & 1 else own) * (1 << i)
        return total_index

    def partner(stage, mask):
        there = {"replica": y, "fsdp": f}
        for i, link in enumerate(stage):
            if mask >> i & 1:
                there[link[0]] = there[link[0]] + (1 - 2 * bit_of(link)) * (1 << link[1])
        return (there["replica"], there["fsdp"])

    def masks(stage):
        return range(1, 1 << len(stage))

    loads = [
        pltpu.make_async_copy(grads, g_buf, load_sem.at[0]),
        pltpu.make_async_copy(errors, e_buf, load_sem.at[1]),
    ]
    for load in loads:
        load.start()

    barrier = pltpu.get_barrier_semaphore()
    peers = [(stage, mask) for stage in reduce_parts[0][2] for mask in masks(stage)]
    for stage, mask in peers:
        pl.semaphore_signal(barrier, inc=1, device_id=partner(stage, mask), device_id_type=MESH)
    held_links = [("fsdp", b) for b in range(nb - 1, -1, -1)]
    if share:
        held_links += [("replica", b) for b in range(nr - 1, -1, -1)]
    piece = held.shape[-1]
    mine = tuple(bit_of(link) for link in held_links)
    first_column = sum(bit_of(link) * (1 << link[1]) for link in held_links if link[0] == "replica") * piece
    if share:
        held[mine] = basis[:, pl.ds(pl.multiple_of(first_column, LANES), piece)]
    else:
        held[mine] = basis[...]
    pl.semaphore_wait(barrier, len(peers))

    def gather(part, step):
        low, high, stages = gather_parts[part]
        done = [link for stage in stages[:step] for link in stage]
        at = tuple(slice(None) if link in done else bit_of(link) for link in held_links)
        at = at + (pl.ds(low, high - low), slice(None))
        out = []
        for mask in masks(stages[step]):
            copy = pltpu.make_async_remote_copy(
                src_ref=held.at[at], dst_ref=held.at[at],
                send_sem=a_send.at[part, step, mask - 1], recv_sem=a_recv.at[part, step, mask - 1],
                device_id=partner(stages[step], mask), device_id_type=MESH,
            )
            copy.start()
            out.append(copy)
        return out

    def factor_tiles(m, free, begin):
        @pl.loop(begin, 1 << len(free))
        def _(j):
            bits = []
            for link in held_links:
                own = bit_of(link)
                if link in free:
                    flip = lax.rem(lax.div(j, 1 << free.index(link)), 2)
                    own = own + flip * (1 - 2 * own)
                bits.append(own)
            start = 0
            for link, value in zip(held_links, bits):
                start = start + value * ((1 << link[1]) * (width if link[0] == "fsdp" else piece))
            here = pl.ds(pl.multiple_of(start, LANES), piece)
            high, low = split(held[tuple(bits) + (pl.ds(m * rank, rank), slice(None))])
            acc[m] += lax.dot_general(
                jnp.concatenate([high, low], axis=0), mhl[m, :, here], NT, preferred_element_type=F32
            )

    copies = [gather(part, 0) for part in range(2)]
    acc[...] = jnp.zeros_like(acc)
    for load in loads:
        load.wait()

    @pl.loop(0, cols // TILE)
    def _(t):
        here = pl.ds(pl.multiple_of(t * TILE, TILE), TILE)
        for m in range(2):
            high, low = split(g_buf[m, :, here].astype(F32) + e_buf[m, :, here])
            mhl[m, 0:rows, here] = high
            mhl[m, rows : 2 * rows, here] = low

    one, two, three = gather_parts[0][2]
    for step in range(3):
        for part in range(2):
            for copy in copies[part]:
                copy.wait()
            if step < 2:
                copies[part] = gather(part, step + 1)
        if step == 0:
            factor_tiles(0, one, 0)
        elif step == 1:
            factor_tiles(0, one + two, 1 << len(one))
            factor_tiles(1, one + two, 0)
        else:
            for m in range(2):
                factor_tiles(m, one + two + three, 1 << len(one + two))

    for m in range(2):
        whole = acc[m, 0:rank] + acc[m, rank : 2 * rank]
        one = whole[:, 0:rows] + whole[:, rows : 2 * rows]
        ft[0, m * rank : (m + 1) * rank] = jnp.concatenate([one, one], axis=1)
    for b in range(nr):
        copy = pltpu.make_async_remote_copy(
            src_ref=ft.at[b], dst_ref=ft_in.at[b], send_sem=f_send.at[b], recv_sem=f_recv.at[b],
            device_id=partner([("replica", b)], 1), device_id_type=MESH,
        )
        copy.start()
        copy.wait()
        ft[b + 1] = ft[b] + ft_in[b]
    factor = ft[nr] * (1.0 / replicas)
    f_high, f_low = split(factor)
    weights = [
        jnp.concatenate([f_high[m * rank : (m + 1) * rank], f_low[m * rank : (m + 1) * rank]], axis=0)
        for m in range(2)
    ]

    def term(m, start, count):
        @pl.loop(0, count // TILE)
        def _(t):
            here = pl.ds(pl.multiple_of(start + t * TILE, TILE), TILE)
            out = lax.dot_general(weights[m], mhl[m, :, here], NN, preferred_element_type=F32)
            z[m * rank : (m + 1) * rank, here] = out[0:rank] + out[rank : 2 * rank]

    half = cols // 2
    core = bit_of(("fsdp", 0))
    parts = range(len(reduce_parts))
    nsteps = 3
    shape = layout(nb, nr, cols)
    starts = [[0] for _ in parts]

    def send(p, step):
        low, high, stages = reduce_parts[p]
        cuts, sizes, offsets = shape[p]
        stage, size, start = stages[step], sizes[step + 1], starts[p][step]
        place = index_of(stage)
        starts[p].append(start + place * size if cuts[step] else start)
        if not cuts[step]:
            own_at = pl.multiple_of(offsets[step] + place * size, LANES)
            z_in[low:high, pl.ds(own_at, size)] = z[low:high, pl.ds(pl.multiple_of(start, LANES), size)]
        out = []
        for mask in masks(stage):
            if cuts[step]:
                away, land = start + index_of(stage, mask) * size, offsets[step] + (mask - 1) * size
            else:
                away, land = start, offsets[step] + place * size
            copy = pltpu.make_async_remote_copy(
                src_ref=z.at[pl.ds(low, high - low), pl.ds(pl.multiple_of(away, LANES), size)],
                dst_ref=z_in.at[pl.ds(low, high - low), pl.ds(pl.multiple_of(land, LANES), size)],
                send_sem=s_send.at[p, step, mask - 1], recv_sem=s_recv.at[p, step, mask - 1],
                device_id=partner(stage, mask), device_id_type=MESH,
            )
            copy.start()
            out.append(copy)
        return out

    def gram_send(step):
        stage = [link for link in reduce_parts[0][2][step] if link[0] == "fsdp"]
        place = index_of(stage)
        gram_in[step, place] = gram[step]
        out = []
        for mask in masks(stage):
            copy = pltpu.make_async_remote_copy(
                src_ref=gram.at[step], dst_ref=gram_in.at[step, place],
                send_sem=m_send.at[step, mask - 1], recv_sem=m_recv.at[step, mask - 1],
                device_id=partner(stage, mask), device_id_type=MESH,
            )
            copy.start()
            out.append(copy)
        return out

    copies = []
    for m in range(2):
        term(m, (1 - core) * half, half)
        copies += [send(p, 0) for p in parts if reduce_parts[p][0] // rank == m]
    product = lax.dot_general(
        factor, jnp.concatenate([factor, factor], axis=0), NT,
        precision=lax.Precision.HIGHEST, preferred_element_type=F32,
    ) * 0.5
    lane = lax.broadcasted_iota(jnp.int32, (rank, LANES), 1)
    gram[0] = jnp.where(lane < rank, product[0:rank], product[rank : 2 * rank])
    g_copies = gram_send(0)
    for m in range(2):
        term(m, core * half, half)
    for step in range(nsteps):
        for p in parts:
            low, high, stages = reduce_parts[p]
            cuts, sizes, offsets = shape[p]
            size = sizes[step + 1]
            for copy in copies[p]:
                copy.wait()
            here = pl.ds(pl.multiple_of(starts[p][step + 1], LANES), size)
            members = 1 << len(stages[step])
            terms = [
                z_in[low:high, offsets[step] + i * size : offsets[step] + (i + 1) * size]
                for i in range(members - cuts[step])
            ]
            added = z[low:high, here] + terms[0] if cuts[step] else terms[0]
            for term_in in terms[1:]:
                added = added + term_in
            if step + 1 < nsteps:
                z[low:high, here] = added
                copies[p] = send(p, step + 1)
            else:
                total[low:high, here] = added
        for copy in g_copies:
            copy.wait()
        members = len(g_copies) + 1
        summed = gram_in[step, 0]
        for i in range(1, members):
            summed = summed + gram_in[step, i]
        gram[step + 1] = summed
        g_copies = gram_send(step + 1) if step + 1 < nsteps else []

    def back(p, step):
        low, high, stages = reduce_parts[p]
        cuts, sizes, _ = shape[p]
        if not cuts[step]:
            return []
        at = (pl.ds(low, high - low), pl.ds(pl.multiple_of(starts[p][step + 1], LANES), sizes[step + 1]))
        out = []
        for mask in masks(stages[step]):
            copy = pltpu.make_async_remote_copy(
                src_ref=total.at[at], dst_ref=total.at[at],
                send_sem=b_send.at[p, step, mask - 1], recv_sem=b_recv.at[p, step, mask - 1],
                device_id=partner(stages[step], mask), device_id_type=MESH,
            )
            copy.start()
            out.append(copy)
        return out

    def advance(step):
        for p in parts:
            for copy in copies[p]:
                copy.wait()
            copies[p] = back(p, step - 1) if step > 0 else []

    copies = [back(p, nsteps - 1) for p in parts]

    row = lax.broadcasted_iota(jnp.int32, (rank, LANES), 0)
    lane = lax.broadcasted_iota(jnp.int32, (rank, LANES), 1)
    first = lax.rem(lane, 2 * rank) < rank
    work = jnp.where(lane < 2 * rank, gram[nsteps], jnp.where(lax.rem(lane, rank) == row, 1.0, 0.0))
    for j in range(rank):
        if j == 12:
            advance(2)
        column = jnp.where(first, work[:, j : j + 1], work[:, rank + j : rank + j + 1])
        top = work[j : j + 1, :] / column[j : j + 1, :]
        work = jnp.where(row > j, work - column * top, work)
    pivots = [
        jnp.sum(jnp.where(lane == row + m * rank, work, 0.0), axis=1, keepdims=True) for m in range(2)
    ]
    scaled = work / jnp.sqrt(jnp.where(first, pivots[0], pivots[1]))
    inv = [scaled[:, (2 + m) * rank : (3 + m) * rank] for m in range(2)]
    for m in range(2):
        solved = lax.dot_general(
            inv[m], factor[m * rank : (m + 1) * rank, 0:rows], NN,
            precision=lax.Precision.HIGHEST, preferred_element_type=F32,
        )
        left_t[m * rank : (m + 1) * rank] = solved
        folded[m] = lax.dot_general(
            solved, inv[m], TN, precision=lax.Precision.HIGHEST, preferred_element_type=F32
        ) * (1.0 / replicas)

    advance(1)
    advance(0)
    own = pl.ds(pl.multiple_of(f * width, LANES), width)
    for m in range(2):
        at = slice(m * rank, (m + 1) * rank)
        own_basis[at] = dot32(inv[m], total[at, own], NN) * (1.0 / replicas)


def finish(grads, errors, total, folded, left_in, basis_in, out, left_out, basis_out):
    rank = total.shape[0] // 2

    @pl.when(pl.program_id(0) == 0)
    def _():
        left_out[...] = left_in[...]
        basis_out[...] = basis_in[...]

    for m in range(2):
        approx = dot32(folded[m], total[m * rank : (m + 1) * rank], NN)
        out[m] = grads[m].astype(F32) + errors[m] - approx


def solution(mesh):
    n, replicas = mesh.shape["fsdp"], mesh.shape["replica"]
    nb, nr = log2(n), log2(replicas)

    def shards(grads, errors, basis):
        _, nmat, rows, cols = grads.shape
        width, _, rank = basis.shape
        grads, errors = grads[0], errors[0]
        basis_t = jnp.transpose(basis, (1, 2, 0)).reshape(nmat * rank, width)
        full = nmat * rank
        share = width // replicas >= LANES
        piece = width // replicas if share else width
        reduce_parts = plan(nb, nr, share)[0]
        nparts, steps = len(reduce_parts), 3
        most = max(1 << len(stage) for stage in reduce_parts[0][2])
        arrivals = max(offsets[-1] for _, _, offsets in layout(nb, nr, cols))
        vmem = pl.BlockSpec(memory_space=pltpu.VMEM)
        hbm = pl.BlockSpec(memory_space=pl.ANY)
        dma = pltpu.SemaphoreType.DMA
        total, left_t, own_basis, folded = pl.pallas_call(
            functools.partial(exchange, n, replicas, share),
            out_shape=[
                jax.ShapeDtypeStruct((full, cols), F32),
                jax.ShapeDtypeStruct((full, rows), F32),
                jax.ShapeDtypeStruct((full, width), F32),
                jax.ShapeDtypeStruct((nmat, rows, rank), F32),
            ],
            in_specs=[hbm, hbm, vmem],
            out_specs=[vmem] * 4,
            scratch_shapes=[
                pltpu.VMEM((2,) * (nb + nr * share) + (full, piece), F32),
                pltpu.VMEM((nmat, rows, cols), BF16),
                pltpu.VMEM((nmat, rows, cols), F32),
                pltpu.VMEM((nmat, 2 * rows, cols), BF16),
                pltpu.VMEM((nmat, 2 * rank, 2 * rows), F32),
                pltpu.VMEM((nr + 1, full, 2 * rows), F32),
                pltpu.VMEM((nr, full, 2 * rows), F32),
                pltpu.VMEM((full, cols), F32),
                pltpu.VMEM((full, arrivals), F32),
                pltpu.VMEM((steps + 1, rank, LANES), F32),
                pltpu.VMEM((steps, most, rank, LANES), F32),
                dma((2,)),
                dma((2, 3, most)), dma((2, 3, most)),
                dma((nr,)), dma((nr,)),
                dma((nparts, steps, most)), dma((nparts, steps, most)),
                dma((steps, most)), dma((steps, most)),
                dma((nparts, steps, most)), dma((nparts, steps, most)),
            ],
            compiler_params=pltpu.CompilerParams(
                collective_id=0, has_side_effects=True, vmem_limit_bytes=60 * 1024 * 1024
            ),
        )(grads, errors, basis_t)

        block = 1024
        whole = lambda a: pl.BlockSpec(a.shape, lambda i: (0,) * a.ndim)
        new_errors, left_t, own_basis = pl.pallas_call(
            finish,
            grid=(cols // block,),
            out_shape=[
                jax.ShapeDtypeStruct((nmat, rows, cols), F32),
                jax.ShapeDtypeStruct(left_t.shape, F32),
                jax.ShapeDtypeStruct(own_basis.shape, F32),
            ],
            in_specs=[
                pl.BlockSpec((nmat, rows, block), lambda i: (0, 0, i)),
                pl.BlockSpec((nmat, rows, block), lambda i: (0, 0, i)),
                pl.BlockSpec((full, block), lambda i: (0, i)),
                whole(folded),
                whole(left_t),
                whole(own_basis),
            ],
            out_specs=[
                pl.BlockSpec((nmat, rows, block), lambda i: (0, 0, i)),
                whole(left_t),
                whole(own_basis),
            ],
            compiler_params=pltpu.CompilerParams(vmem_limit_bytes=60 * 1024 * 1024),
        )(grads, errors, total, folded, left_t, own_basis)
        left = jnp.transpose(left_t.reshape(nmat, rank, rows), (0, 2, 1))
        new_basis = jnp.transpose(own_basis.reshape(nmat, rank, width), (2, 0, 1))
        return (new_errors[None], left, new_basis)

    in_specs = (
        P("replica", None, "fsdp", None),
        P("replica", None, "fsdp", None),
        P("fsdp", None, None),
    )
    out_specs = (P("replica", None, "fsdp", None), P(None, "fsdp", None), P("fsdp", None, None))
    return jax.shard_map(shards, mesh=mesh, in_specs=in_specs, out_specs=out_specs, check_vma=False)
```

time: 85.7 us -> 82.3 us (0.960)
  Pallas kernels: 83.4 us -> 81 us
  local copies, waits for them, and re-layouts: 1.28 us -> 0 us
    pallas_call x2, Pallas kernels: 83.4 us -> 81 us  [the longest x1 72.5 us: shards(): pl.pallas_call(functools.partial(exchange, n, replicas, share), out_shape...]
    unnamed x6 -> x0, local copies, waits for them, and re-layouts: 1.28 us -> none
where the time goes in v3:
time: 82.3 us; the launch traced here: 81.6 us
  Pallas kernels  81 us (98%)
    pallas_call x1, Pallas kernels, shards(): pl.pallas_call(functools.partial(exchange, n, replicas, share), out_shape...  72.5 us
    pallas_call x1, Pallas kernels, shards(): pl.pallas_call(finish, grid=(cols // block,), out_shape=[jax.ShapeDtypeSt...  8.5 us

profile of v3, /device:TPU:0, one launch (start us, length us, event | category | flops | bytes accessed | tf_op | source)
XLA Modules:
  0.0 81.6 jit_solution(13780710604306984781)
XLA Ops:
  0.6 72.5 %shard_map.58 = (f32[64,8192]{1,0:T(8,128)}, f32[64,64]{1,0:T(8,128)}, f32[64,512]{1,0:T(8,128)}, f32[2,64,32]{2,1,0:T(8,128)}) custom-call(bf16[2,64,8192]{2,1,0:T(8,128)(2,1)} %bitcast.14, f32[2,64,8192]{2,1,0:T(8,128)} %bitcast.12, f32[64,512]{1,0:T(8,128)} %bitcast.16), custom_call_target="tpu_custom_call" | custom-call | tf_op jit(solution)/shard_map/pallas_call | solution.py:391
  73.1 8.5 %shard_map.59 = (f32[2,64,8192]{2,1,0:T(8,128)}, f32[64,64]{1,0:T(8,128)}, f32[64,512]{1,0:T(8,128)}) custom-call(bf16[2,64,8192]{2,1,0:T(8,128)(2,1)} %bitcast.15, f32[2,64,8192]{2,1,0:T(8,128)} %bitcast.13, f32[64,8192]{1,0:T(8,128)} %get-tuple-element.10.total, f32[2,64,32]{2,1,0:T(8,128)} %get-tuple-element.11.folded, ...), custom_call_target="tpu_custom_call" | custom-call | tf_op jit(solution)/shard_map/pallas_call | solution.py:427

commit v4 on v3

--- a/solution.py
+++ b/solution.py
@@ -63,8 +63,8 @@
 
 
 def exchange(
-    n, replicas, share, grads, errors, basis, total, left_t, own_basis, folded,
-    held, g_buf, e_buf, mhl, acc, ft, ft_in, z, z_in, gram, gram_in,
+    n, replicas, share, grads, errors, basis, merged, total, left_t, own_basis, folded,
+    held, g_buf, mhl, acc, ft, ft_in, z, z_in, gram, gram_in,
     load_sem, a_send, a_recv, f_send, f_recv, s_send, s_recv, m_send, m_recv, b_send, b_recv,
 ):
     nb, nr = log2(n), log2(replicas)
@@ -97,7 +97,7 @@
 
     loads = [
         pltpu.make_async_copy(grads, g_buf, load_sem.at[0]),
-        pltpu.make_async_copy(errors, e_buf, load_sem.at[1]),
+        pltpu.make_async_copy(errors, merged, load_sem.at[1]),
     ]
     for load in loads:
         load.start()
@@ -135,23 +135,30 @@
         return out
 
     def factor_tiles(m, free, begin):
-        @pl.loop(begin, 1 << len(free))
-        def _(j):
-            bits = []
-            for link in held_links:
-                own = bit_of(link)
-                if link in free:
-                    flip = lax.rem(lax.div(j, 1 << free.index(link)), 2)
-                    own = own + flip * (1 - 2 * own)
-                bits.append(own)
-            start = 0
-            for link, value in zip(held_links, bits):
-                start = start + value * ((1 << link[1]) * (width if link[0] == "fsdp" else piece))
-            here = pl.ds(pl.multiple_of(start, LANES), piece)
-            high, low = split(held[tuple(bits) + (pl.ds(m * rank, rank), slice(None))])
-            acc[m] += lax.dot_general(
-                jnp.concatenate([high, low], axis=0), mhl[m, :, here], NT, preferred_element_type=F32
-            )
+        end = 1 << len(free)
+        group = 8 if begin % 8 == 0 and end % 8 == 0 else 4
+
+        @pl.loop(begin // group, end // group)
+        def _(outer):
+            summed = 0.0
+            for inner in range(group):
+                j = outer * group + inner
+                bits = []
+                for link in held_links:
+                    own = bit_of(link)
+                    if link in free:
+                        flip = lax.rem(lax.div(j, 1 << free.index(link)), 2)
+                        own = own + flip * (1 - 2 * own)
+                    bits.append(own)
+                start = 0
+                for link, value in zip(held_links, bits):
+                    start = start + value * ((1 << link[1]) * (width if link[0] == "fsdp" else piece))
+                here = pl.ds(pl.multiple_of(start, LANES), piece)
+                high, low = split(held[tuple(bits) + (pl.ds(m * rank, rank), slice(None))])
+                summed = summed + lax.dot_general(
+                    jnp.concatenate([high, low], axis=0), mhl[m, :, here], NT, preferred_element_type=F32
+                )
+            acc[m] += summed
 
     copies = [gather(part, 0) for part in range(2)]
     acc[...] = jnp.zeros_like(acc)
@@ -162,7 +169,9 @@
     def _(t):
         here = pl.ds(pl.multiple_of(t * TILE, TILE), TILE)
         for m in range(2):
-            high, low = split(g_buf[m, :, here].astype(F32) + e_buf[m, :, here])
+            both = g_buf[m, :, here].astype(F32) + merged[m, :, here]
+            merged[m, :, here] = both
+            high, low = split(both)
             mhl[m, 0:rows, here] = high
             mhl[m, rows : 2 * rows, here] = low
 
@@ -202,9 +211,9 @@
     ]
 
     def term(m, start, count):
-        @pl.loop(0, count // TILE)
+        @pl.loop(0, count // (2 * TILE))
         def _(t):
-            here = pl.ds(pl.multiple_of(start + t * TILE, TILE), TILE)
+            here = pl.ds(pl.multiple_of(start + t * 2 * TILE, 2 * TILE), 2 * TILE)
             out = lax.dot_general(weights[m], mhl[m, :, here], NN, preferred_element_type=F32)
             z[m * rank : (m + 1) * rank, here] = out[0:rank] + out[rank : 2 * rank]
 
@@ -356,8 +365,10 @@
         own_basis[at] = dot32(inv[m], total[at, own], NN) * (1.0 / replicas)
 
 
-def finish(grads, errors, total, folded, left_in, basis_in, out, left_out, basis_out):
+def finish(merged, total, folded, left_in, basis_in, out, left_out, basis_out):
     rank = total.shape[0] // 2
+    block = out.shape[2]
+    here = pl.ds(pl.multiple_of(pl.program_id(0) * block, block), block)
 
     @pl.when(pl.program_id(0) == 0)
     def _():
@@ -365,8 +376,8 @@
         basis_out[...] = basis_in[...]
 
     for m in range(2):
-        approx = dot32(folded[m], total[m * rank : (m + 1) * rank], NN)
-        out[m] = grads[m].astype(F32) + errors[m] - approx
+        approx = dot32(folded[m], total[m * rank : (m + 1) * rank, here], NN)
+        out[m] = merged[m, :, here] - approx
 
 
 def solution(mesh):
@@ -386,22 +397,22 @@
         most = max(1 << len(stage) for stage in reduce_parts[0][2])
         arrivals = max(offsets[-1] for _, _, offsets in layout(nb, nr, cols))
         vmem = pl.BlockSpec(memory_space=pltpu.VMEM)
-        hbm = pl.BlockSpec(memory_space=pl.ANY)
+        hbm = pl.BlockSpec(memory_space=pltpu.HBM)
         dma = pltpu.SemaphoreType.DMA
-        total, left_t, own_basis, folded = pl.pallas_call(
+        merged, total, left_t, own_basis, folded = pl.pallas_call(
             functools.partial(exchange, n, replicas, share),
             out_shape=[
-                jax.ShapeDtypeStruct((full, cols), F32),
-                jax.ShapeDtypeStruct((full, rows), F32),
-                jax.ShapeDtypeStruct((full, width), F32),
-                jax.ShapeDtypeStruct((nmat, rows, rank), F32),
+                pltpu.VMEM((nmat, rows, cols), F32),
+                pltpu.VMEM((full, cols), F32),
+                pltpu.VMEM((full, rows), F32),
+                pltpu.VMEM((full, width), F32),
+                pltpu.VMEM((nmat, rows, rank), F32),
             ],
             in_specs=[hbm, hbm, vmem],
-            out_specs=[vmem] * 4,
+            out_specs=[vmem] * 5,
             scratch_shapes=[
                 pltpu.VMEM((2,) * (nb + nr * share) + (full, piece), F32),
                 pltpu.VMEM((nmat, rows, cols), BF16),
-                pltpu.VMEM((nmat, rows, cols), F32),
                 pltpu.VMEM((nmat, 2 * rows, cols), BF16),
                 pltpu.VMEM((nmat, 2 * rank, 2 * rows), F32),
                 pltpu.VMEM((nr + 1, full, 2 * rows), F32),
@@ -418,7 +429,7 @@
                 dma((nparts, steps, most)), dma((nparts, steps, most)),
             ],
             compiler_params=pltpu.CompilerParams(
-                collective_id=0, has_side_effects=True, vmem_limit_bytes=60 * 1024 * 1024
+                collective_id=0, has_side_effects=True, vmem_limit_bytes=56 * 1024 * 1024
             ),
         )(grads, errors, basis_t)
 
@@ -433,20 +444,19 @@
                 jax.ShapeDtypeStruct(own_basis.shape, F32),
             ],
             in_specs=[
-                pl.BlockSpec((nmat, rows, block), lambda i: (0, 0, i)),
-                pl.BlockSpec((nmat, rows, block), lambda i: (0, 0, i)),
-                pl.BlockSpec((full, block), lambda i: (0, i)),
-                whole(folded),
-                whole(left_t),
-                whole(own_basis),
+                vmem,
+                vmem,
+                vmem,
+                vmem,
+                vmem,
             ],
             out_specs=[
                 pl.BlockSpec((nmat, rows, block), lambda i: (0, 0, i)),
                 whole(left_t),
                 whole(own_basis),
             ],
-            compiler_params=pltpu.CompilerParams(vmem_limit_bytes=60 * 1024 * 1024),
-        )(grads, errors, total, folded, left_t, own_basis)
+            compiler_params=pltpu.CompilerParams(vmem_limit_bytes=24 * 1024 * 1024),
+        )(merged, total, folded, left_t, own_basis)
         left = jnp.transpose(left_t.reshape(nmat, rank, rows), (0, 2, 1))
         new_basis = jnp.transpose(own_basis.reshape(nmat, rank, width), (2, 0, 1))
         return (new_errors[None], left, new_basis)

time: 82.3 us -> 67.3 us (0.82)
  Pallas kernels: 81 us -> 66.5 us
    pallas_call x1, Pallas kernels: 72.5 us -> 61.9 us  [shards(): pl.pallas_call(functools.partial(exchange, n, replicas, share), out_shape...]
    pallas_call x1, Pallas kernels: 8.5 us -> 4.59 us  [shards(): pl.pallas_call(finish, grid=(cols // block,), out_shape=[jax.ShapeDtypeSt...]
where the time goes in v4:
time: 67.3 us; the launch traced here: 67.1 us
  Pallas kernels  66.5 us (99%)
    pallas_call x1, Pallas kernels, shards(): pl.pallas_call(functools.partial(exchange, n, replicas, share), out_shape...  61.9 us
    pallas_call x1, Pallas kernels, shards(): pl.pallas_call(finish, grid=(cols // block,), out_shape=[jax.ShapeDtypeSt...  4.59 us

profile of v4, /device:TPU:0, one launch (start us, length us, event | category | flops | bytes accessed | tf_op | source)
XLA Modules:
  0.0 67.1 jit_solution(6549965908999044968)
XLA Ops:
  0.6 61.9 %shard_map.58 = (f32[2,64,8192]{2,1,0:T(8,128)S(1)}, f32[64,8192]{1,0:T(8,128)S(1)}, f32[64,64]{1,0:T(8,128)S(1)}, f32[64,512]{1,0:T(8,128)S(1)}, f32[2,64,32]{2,1,0:T(8,128)S(1)}) custom-call(bf16[2,64,8192]{2,1,0:T(8,128)(2,1)} %bitcast.13, f32[2,64,8192]{2,1,0:T(8,128)} %bitcast.12, f32[64,512]{1,0:T(8,128)} %bitcast.14), custom_call_target="tpu_custom_call" | custom-call | tf_op jit(solution)/shard_map/pallas_call | solution.py:402
  62.5 4.6 %shard_map.59 = (f32[2,64,8192]{2,1,0:T(8,128)}, f32[64,64]{1,0:T(8,128)}, f32[64,512]{1,0:T(8,128)}) custom-call(f32[2,64,8192]{2,1,0:T(8,128)S(1)} %get-tuple-element.11.merged, f32[64,8192]{1,0:T(8,128)S(1)} %get-tuple-element.12.total, f32[2,64,32]{2,1,0:T(8,128)S(1)} %get-tuple-element.13.folded, f32[64,64]{1,0:T(8,128)S(1)} %get-tuple-element.14.left_in, ...), custom_call_target="tpu_custom_call" | custom-call | tf_op jit(solution)/shard_map/pallas_call | solution.py:438

commit v5 on v4

--- a/solution.py
+++ b/solution.py
@@ -96,10 +96,13 @@
         return range(1, 1 << len(stage))
 
     loads = [
-        pltpu.make_async_copy(grads, g_buf, load_sem.at[0]),
-        pltpu.make_async_copy(errors, merged, load_sem.at[1]),
+        [
+            pltpu.make_async_copy(grads.at[m], g_buf.at[m], load_sem.at[m, 0]),
+            pltpu.make_async_copy(errors.at[m], merged.at[m], load_sem.at[m, 1]),
+        ]
+        for m in range(2)
     ]
-    for load in loads:
+    for load in loads[0] + loads[1]:
         load.start()
 
     barrier = pltpu.get_barrier_semaphore()
@@ -162,13 +165,14 @@
 
     copies = [gather(part, 0) for part in range(2)]
     acc[...] = jnp.zeros_like(acc)
-    for load in loads:
-        load.wait()
-
-    @pl.loop(0, cols // TILE)
-    def _(t):
-        here = pl.ds(pl.multiple_of(t * TILE, TILE), TILE)
-        for m in range(2):
+
+    def convert(m):
+        for load in loads[m]:
+            load.wait()
+
+        @pl.loop(0, cols // (2 * TILE))
+        def _(t):
+            here = pl.ds(pl.multiple_of(t * 2 * TILE, 2 * TILE), 2 * TILE)
             both = g_buf[m, :, here].astype(F32) + merged[m, :, here]
             merged[m, :, here] = both
             high, low = split(both)
@@ -176,45 +180,58 @@
             mhl[m, rows : 2 * rows, here] = low
 
     one, two, three = gather_parts[0][2]
-    for step in range(3):
-        for part in range(2):
-            for copy in copies[part]:
-                copy.wait()
-            if step < 2:
-                copies[part] = gather(part, step + 1)
-        if step == 0:
-            factor_tiles(0, one, 0)
-        elif step == 1:
-            factor_tiles(0, one + two, 1 << len(one))
-            factor_tiles(1, one + two, 0)
-        else:
-            for m in range(2):
-                factor_tiles(m, one + two + three, 1 << len(one + two))
-
-    for m in range(2):
-        whole = acc[m, 0:rank] + acc[m, rank : 2 * rank]
-        one = whole[:, 0:rows] + whole[:, rows : 2 * rows]
-        ft[0, m * rank : (m + 1) * rank] = jnp.concatenate([one, one], axis=1)
-    for b in range(nr):
+
+    def arrive(part, step):
+        for copy in copies[part]:
+            copy.wait()
+        copies[part] = gather(part, step + 1) if step < 2 else []
+
+    def factor_send(m, b):
         copy = pltpu.make_async_remote_copy(
-            src_ref=ft.at[b], dst_ref=ft_in.at[b], send_sem=f_send.at[b], recv_sem=f_recv.at[b],
+            src_ref=ft.at[b, m], dst_ref=ft_in.at[b, m],
+            send_sem=f_send.at[b, m], recv_sem=f_recv.at[b, m],
             device_id=partner([("replica", b)], 1), device_id_type=MESH,
         )
         copy.start()
-        copy.wait()
-        ft[b + 1] = ft[b] + ft_in[b]
-    factor = ft[nr] * (1.0 / replicas)
-    f_high, f_low = split(factor)
-    weights = [
-        jnp.concatenate([f_high[m * rank : (m + 1) * rank], f_low[m * rank : (m + 1) * rank]], axis=0)
-        for m in range(2)
-    ]
+        return copy
+
+    def factor_first(m):
+        factor_tiles(m, one + two + three, 1 << len(one + two))
+        whole = acc[m, 0:rank] + acc[m, rank : 2 * rank]
+        single = whole[:, 0:rows] + whole[:, rows : 2 * rows]
+        ft[0, m] = jnp.concatenate([single, single], axis=1)
+        return factor_send(m, 0)
+
+    def factor_last(m, copy):
+        for b in range(nr):
+            copy.wait()
+            ft[b + 1, m] = ft[b, m] + ft_in[b, m]
+            if b + 1 < nr:
+                copy = factor_send(m, b + 1)
+        return ft[nr, m] * (1.0 / replicas)
+
+    convert(0)
+    for part in range(2):
+        arrive(part, 0)
+    convert(1)
+    factor_tiles(0, one, 0)
+    for part in range(2):
+        arrive(part, 1)
+    factor_tiles(0, one + two, 1 << len(one))
+    factor_tiles(1, one + two, 0)
+    arrive(0, 2)
+    f_copies = [factor_first(0)]
+    arrive(1, 2)
+    f_copies.append(factor_first(1))
 
     def term(m, start, count):
-        @pl.loop(0, count // (2 * TILE))
+        high, low = split(factors[m])
+        weights = jnp.concatenate([high, low], axis=0)
+
+        @pl.loop(0, count // (4 * TILE))
         def _(t):
-            here = pl.ds(pl.multiple_of(start + t * 2 * TILE, 2 * TILE), 2 * TILE)
-            out = lax.dot_general(weights[m], mhl[m, :, here], NN, preferred_element_type=F32)
+            here = pl.ds(pl.multiple_of(start + t * 4 * TILE, 4 * TILE), 4 * TILE)
+            out = lax.dot_general(weights, mhl[m, :, here], NN, preferred_element_type=F32)
             z[m * rank : (m + 1) * rank, here] = out[0:rank] + out[rank : 2 * rank]
 
     half = cols // 2
@@ -265,9 +282,12 @@
         return out
 
     copies = []
+    factors = []
     for m in range(2):
+        factors.append(factor_last(m, f_copies[m]))
         term(m, (1 - core) * half, half)
         copies += [send(p, 0) for p in parts if reduce_parts[p][0] // rank == m]
+    factor = jnp.concatenate(factors, axis=0)
     product = lax.dot_general(
         factor, jnp.concatenate([factor, factor], axis=0), NT,
         precision=lax.Precision.HIGHEST, preferred_element_type=F32,
@@ -415,15 +435,15 @@
                 pltpu.VMEM((nmat, rows, cols), BF16),
                 pltpu.VMEM((nmat, 2 * rows, cols), BF16),
                 pltpu.VMEM((nmat, 2 * rank, 2 * rows), F32),
-                pltpu.VMEM((nr + 1, full, 2 * rows), F32),
-                pltpu.VMEM((nr, full, 2 * rows), F32),
+                pltpu.VMEM((nr + 1, nmat, rank, 2 * rows), F32),
+                pltpu.VMEM((nr, nmat, rank, 2 * rows), F32),
                 pltpu.VMEM((full, cols), F32),
                 pltpu.VMEM((full, arrivals), F32),
                 pltpu.VMEM((steps + 1, rank, LANES), F32),
                 pltpu.VMEM((steps, most, rank, LANES), F32),
-                dma((2,)),
+                dma((nmat, 2)),
                 dma((2, 3, most)), dma((2, 3, most)),
-                dma((nr,)), dma((nr,)),
+                dma((nr, nmat)), dma((nr, nmat)),
                 dma((nparts, steps, most)), dma((nparts, steps, most)),
                 dma((steps, most)), dma((steps, most)),
                 dma((nparts, steps, most)), dma((nparts, steps, most)),

time: 67.3 us -> 65.8 us (0.978)
  Pallas kernels: 66.5 us -> 65 us
    pallas_call x1, Pallas kernels: 61.9 us -> 60.4 us  [shards(): pl.pallas_call(functools.partial(exchange, n, replicas, share), out_shape...]
where the time goes in v5:
time: 65.8 us; the launch traced here: 65.6 us
  Pallas kernels  65 us (99%)
    pallas_call x1, Pallas kernels, shards(): pl.pallas_call(functools.partial(exchange, n, replicas, share), out_shape...  60.4 us
    pallas_call x1, Pallas kernels, shards(): pl.pallas_call(finish, grid=(cols // block,), out_shape=[jax.ShapeDtypeSt...  4.57 us

profile of v5, /device:TPU:0, one launch (start us, length us, event | category | flops | bytes accessed | tf_op | source)
XLA Modules:
  0.0 65.6 jit_solution(3036562064043480318)
XLA Ops:
  0.6 60.4 %shard_map.58 = (f32[2,64,8192]{2,1,0:T(8,128)S(1)}, f32[64,8192]{1,0:T(8,128)S(1)}, f32[64,64]{1,0:T(8,128)S(1)}, f32[64,512]{1,0:T(8,128)S(1)}, f32[2,64,32]{2,1,0:T(8,128)S(1)}) custom-call(bf16[2,64,8192]{2,1,0:T(8,128)(2,1)} %bitcast.13, f32[2,64,8192]{2,1,0:T(8,128)} %bitcast.12, f32[64,512]{1,0:T(8,128)} %bitcast.14), custom_call_target="tpu_custom_call" | custom-call | tf_op jit(solution)/shard_map/pallas_call | solution.py:422
  61.0 4.6 %shard_map.59 = (f32[2,64,8192]{2,1,0:T(8,128)}, f32[64,64]{1,0:T(8,128)}, f32[64,512]{1,0:T(8,128)}) custom-call(f32[2,64,8192]{2,1,0:T(8,128)S(1)} %get-tuple-element.11.merged, f32[64,8192]{1,0:T(8,128)S(1)} %get-tuple-element.12.total, f32[2,64,32]{2,1,0:T(8,128)S(1)} %get-tuple-element.13.folded, f32[64,64]{1,0:T(8,128)S(1)} %get-tuple-element.14.left_in, ...), custom_call_target="tpu_custom_call" | custom-call | tf_op jit(solution)/shard_map/pallas_call | solution.py:458

commit v6 on v5

--- a/solution.py
+++ b/solution.py
@@ -121,21 +121,34 @@
         held[mine] = basis[...]
     pl.semaphore_wait(barrier, len(peers))
 
+    def gather_copy(part, step, at, mask, slot):
+        low, high, stages = gather_parts[part]
+        ref = held.at[at + (pl.ds(low, high - low), slice(None))]
+        copy = pltpu.make_async_remote_copy(
+            src_ref=ref, dst_ref=ref,
+            send_sem=a_send.at[part, step, slot], recv_sem=a_recv.at[part, step, slot],
+            device_id=partner(stages[step], mask), device_id_type=MESH,
+        )
+        copy.start()
+        return copy
+
     def gather(part, step):
-        low, high, stages = gather_parts[part]
+        stages = gather_parts[part][2]
         done = [link for stage in stages[:step] for link in stage]
         at = tuple(slice(None) if link in done else bit_of(link) for link in held_links)
-        at = at + (pl.ds(low, high - low), slice(None))
-        out = []
-        for mask in masks(stages[step]):
-            copy = pltpu.make_async_remote_copy(
-                src_ref=held.at[at], dst_ref=held.at[at],
-                send_sem=a_send.at[part, step, mask - 1], recv_sem=a_recv.at[part, step, mask - 1],
-                device_id=partner(stages[step], mask), device_id_type=MESH,
-            )
-            copy.start()
-            out.append(copy)
-        return out
+        return [gather_copy(part, step, at, mask, mask - 1) for mask in masks(stages[step])]
+
+    def pass_on(part, mask):
+        first_stage, second_stage, _ = gather_parts[part][2]
+        at = []
+        for link in held_links:
+            own = bit_of(link)
+            if link in first_stage:
+                own = slice(None)
+            elif link in second_stage and mask >> second_stage.index(link) & 1:
+                own = 1 - own
+            at.append(own)
+        return gather_copy(part, 2, tuple(at), 1, mask)
 
     def factor_tiles(m, free, begin):
         end = 1 << len(free)
@@ -181,10 +194,23 @@
 
     one, two, three = gather_parts[0][2]
 
+    passed = [[], []]
+
     def arrive(part, step):
-        for copy in copies[part]:
-            copy.wait()
-        copies[part] = gather(part, step + 1) if step < 2 else []
+        if step == 0:
+            for copy in copies[part]:
+                copy.wait()
+            copies[part] = gather(part, 1)
+            passed[part].append(pass_on(part, 0))
+        elif step == 1:
+            for mask, copy in enumerate(copies[part], 1):
+                copy.wait_recv()
+                passed[part].append(pass_on(part, mask))
+            for copy in copies[part]:
+                copy.wait_send()
+        else:
+            for copy in passed[part]:
+                copy.wait()
 
     def factor_send(m, b):
         copy = pltpu.make_async_remote_copy(
@@ -327,28 +353,46 @@
         gram[step + 1] = summed
         g_copies = gram_send(step + 1) if step + 1 < nsteps else []
 
+    def back_copy(p, step, start, size, mask, slot):
+        low, high, stages = reduce_parts[p]
+        ref = total.at[pl.ds(low, high - low), pl.ds(pl.multiple_of(start, LANES), size)]
+        copy = pltpu.make_async_remote_copy(
+            src_ref=ref, dst_ref=ref,
+            send_sem=b_send.at[p, step, slot], recv_sem=b_recv.at[p, step, slot],
+            device_id=partner(stages[step], mask), device_id_type=MESH,
+        )
+        copy.start()
+        return copy
+
     def back(p, step):
-        low, high, stages = reduce_parts[p]
         cuts, sizes, _ = shape[p]
         if not cuts[step]:
             return []
-        at = (pl.ds(low, high - low), pl.ds(pl.multiple_of(starts[p][step + 1], LANES), sizes[step + 1]))
-        out = []
-        for mask in masks(stages[step]):
-            copy = pltpu.make_async_remote_copy(
-                src_ref=total.at[at], dst_ref=total.at[at],
-                send_sem=b_send.at[p, step, mask - 1], recv_sem=b_recv.at[p, step, mask - 1],
-                device_id=partner(stages[step], mask), device_id_type=MESH,
-            )
-            copy.start()
-            out.append(copy)
-        return out
+        return [
+            back_copy(p, step, starts[p][step + 1], sizes[step + 1], mask, mask - 1)
+            for mask in masks(reduce_parts[p][2][step])
+        ]
+
+    handed = [[] for _ in parts]
 
     def advance(step):
         for p in parts:
-            for copy in copies[p]:
-                copy.wait()
-            copies[p] = back(p, step - 1) if step > 0 else []
+            sizes, stages = shape[p][1], reduce_parts[p][2]
+            if step == 2:
+                for copy in copies[p]:
+                    copy.wait()
+                copies[p] = back(p, 1)
+                handed[p].append(back_copy(p, 0, starts[p][2], sizes[2], 1, 0))
+            elif step == 1:
+                for mask, copy in enumerate(copies[p], 1):
+                    copy.wait_recv()
+                    start = starts[p][1] + index_of(stages[1], mask) * sizes[2]
+                    handed[p].append(back_copy(p, 0, start, sizes[2], 1, mask))
+                for copy in copies[p]:
+                    copy.wait_send()
+            else:
+                for copy in handed[p]:
+                    copy.wait()
 
     copies = [back(p, nsteps - 1) for p in parts]
 

time: 65.8 us -> 65.6 us (level)
  no operation moved by 1% of the time
where the time goes in v6:
time: 65.6 us; the launch traced here: 65.5 us
  Pallas kernels  64.9 us (99%)
    pallas_call x1, Pallas kernels, shards(): pl.pallas_call(functools.partial(exchange, n, replicas, share), out_shape...  60.3 us
    pallas_call x1, Pallas kernels, shards(): pl.pallas_call(finish, grid=(cols // block,), out_shape=[jax.ShapeDtypeSt...  4.59 us

profile of v6, /device:TPU:0, one launch (start us, length us, event | category | flops | bytes accessed | tf_op | source)
XLA Modules:
  0.0 65.5 jit_solution(14365236020934508029)
XLA Ops:
  0.6 60.3 %shard_map.58 = (f32[2,64,8192]{2,1,0:T(8,128)S(1)}, f32[64,8192]{1,0:T(8,128)S(1)}, f32[64,64]{1,0:T(8,128)S(1)}, f32[64,512]{1,0:T(8,128)S(1)}, f32[2,64,32]{2,1,0:T(8,128)S(1)}) custom-call(bf16[2,64,8192]{2,1,0:T(8,128)(2,1)} %bitcast.13, f32[2,64,8192]{2,1,0:T(8,128)} %bitcast.12, f32[64,512]{1,0:T(8,128)} %bitcast.14), custom_call_target="tpu_custom_call" | custom-call | tf_op jit(solution)/shard_map/pallas_call | solution.py:466
  60.9 4.6 %shard_map.59 = (f32[2,64,8192]{2,1,0:T(8,128)}, f32[64,64]{1,0:T(8,128)}, f32[64,512]{1,0:T(8,128)}) custom-call(f32[2,64,8192]{2,1,0:T(8,128)S(1)} %get-tuple-element.11.merged, f32[64,8192]{1,0:T(8,128)S(1)} %get-tuple-element.12.total, f32[2,64,32]{2,1,0:T(8,128)S(1)} %get-tuple-element.13.folded, f32[64,64]{1,0:T(8,128)S(1)} %get-tuple-element.14.left_in, ...), custom_call_target="tpu_custom_call" | custom-call | tf_op jit(solution)/shard_map/pallas_call | solution.py:502

commit v7 on v6

--- a/solution.py
+++ b/solution.py
@@ -38,11 +38,12 @@
     core, near = [("fsdp", 0)], [("fsdp", 1)]
     far = [("fsdp", b) for b in range(2, nb)]
     across = [("replica", b) for b in range(nr)]
-    plane_first = [core, near + across, far]
-    far_first = [core, far, near + across]
+    x_first = [core, near, across, far]
+    y_first = [core, across, near, far]
+    z_first = [core, far[:1], far[1:], near + across]
     reduce_parts = [
-        (0, 16, plane_first), (16, 32, plane_first), (32, 40, plane_first),
-        (40, 48, far_first), (48, 64, far_first),
+        (0, 8, x_first), (8, 24, x_first), (24, 32, z_first),
+        (32, 40, z_first), (40, 48, y_first), (48, 64, y_first),
     ]
     plane = near + across if share else near
     gather_parts = [(0, 40, [far, plane, core]), (40, 64, [plane, far, core])]
@@ -106,7 +107,8 @@
         load.start()
 
     barrier = pltpu.get_barrier_semaphore()
-    peers = [(stage, mask) for stage in reduce_parts[0][2] for mask in masks(stage)]
+    groups = [[("fsdp", 0)], [("fsdp", 1)] + [("replica", b) for b in range(nr)], [("fsdp", b) for b in range(2, nb)]]
+    peers = [(group, mask) for group in groups for mask in masks(group)]
     for stage, mask in peers:
         pl.semaphore_signal(barrier, inc=1, device_id=partner(stage, mask), device_id_type=MESH)
     held_links = [("fsdp", b) for b in range(nb - 1, -1, -1)]
@@ -263,7 +265,7 @@
     half = cols // 2
     core = bit_of(("fsdp", 0))
     parts = range(len(reduce_parts))
-    nsteps = 3
+    nsteps = len(reduce_parts[0][2])
     shape = layout(nb, nr, cols)
     starts = [[0] for _ in parts]
 
@@ -375,33 +377,35 @@
 
     handed = [[] for _ in parts]
 
+    def hand(p, start, size):
+        handed[p].append(back_copy(p, 0, start, size, 1, len(handed[p])))
+
     def advance(step):
         for p in parts:
             sizes, stages = shape[p][1], reduce_parts[p][2]
-            if step == 2:
-                for copy in copies[p]:
-                    copy.wait()
-                copies[p] = back(p, 1)
-                handed[p].append(back_copy(p, 0, starts[p][2], sizes[2], 1, 0))
-            elif step == 1:
-                for mask, copy in enumerate(copies[p], 1):
-                    copy.wait_recv()
-                    start = starts[p][1] + index_of(stages[1], mask) * sizes[2]
-                    handed[p].append(back_copy(p, 0, start, sizes[2], 1, mask))
-                for copy in copies[p]:
-                    copy.wait_send()
-            else:
+            if step == 0:
                 for copy in handed[p]:
                     copy.wait()
+                continue
+            for mask, copy in enumerate(copies[p], 1):
+                copy.wait_recv()
+                hand(p, starts[p][step] + index_of(stages[step], mask) * sizes[step + 1], sizes[step + 1])
+            for copy in copies[p]:
+                copy.wait_send()
+            copies[p] = back(p, step - 1) if step > 1 else []
 
     copies = [back(p, nsteps - 1) for p in parts]
+    for p in parts:
+        hand(p, starts[p][nsteps], shape[p][1][nsteps])
 
     row = lax.broadcasted_iota(jnp.int32, (rank, LANES), 0)
     lane = lax.broadcasted_iota(jnp.int32, (rank, LANES), 1)
     first = lax.rem(lane, 2 * rank) < rank
     work = jnp.where(lane < 2 * rank, gram[nsteps], jnp.where(lax.rem(lane, rank) == row, 1.0, 0.0))
     for j in range(rank):
-        if j == 12:
+        if j == 10:
+            advance(3)
+        if j == 22:
             advance(2)
         column = jnp.where(first, work[:, j : j + 1], work[:, rank + j : rank + j + 1])
         top = work[j : j + 1, :] / column[j : j + 1, :]
@@ -457,8 +461,8 @@
         share = width // replicas >= LANES
         piece = width // replicas if share else width
         reduce_parts = plan(nb, nr, share)[0]
-        nparts, steps = len(reduce_parts), 3
-        most = max(1 << len(stage) for stage in reduce_parts[0][2])
+        nparts, steps = len(reduce_parts), len(reduce_parts[0][2])
+        most = max(sum(1 << len(stage) for stage in stages) for _, _, stages in reduce_parts)
         arrivals = max(offsets[-1] for _, _, offsets in layout(nb, nr, cols))
         vmem = pl.BlockSpec(memory_space=pltpu.VMEM)
         hbm = pl.BlockSpec(memory_space=pltpu.HBM)

time: 65.6 us -> 75.6 us (1.15)
  Pallas kernels: 64.9 us -> 74.8 us
    pallas_call x1, Pallas kernels: 60.3 us -> 70.2 us  [shards(): pl.pallas_call(functools.partial(exchange, n, replicas, share), out_shape...]
where the time goes in v7:
time: 75.6 us; the launch traced here: 75.4 us
  Pallas kernels  74.8 us (99%)
    pallas_call x1, Pallas kernels, shards(): pl.pallas_call(functools.partial(exchange, n, replicas, share), out_shape...  70.2 us
    pallas_call x1, Pallas kernels, shards(): pl.pallas_call(finish, grid=(cols // block,), out_shape=[jax.ShapeDtypeSt...  4.57 us

profile of v7, /device:TPU:0, one launch (start us, length us, event | category | flops | bytes accessed | tf_op | source)
XLA Modules:
  0.0 75.4 jit_solution(1491607696963949949)
XLA Ops:
  0.6 70.2 %shard_map.58 = (f32[2,64,8192]{2,1,0:T(8,128)S(1)}, f32[64,8192]{1,0:T(8,128)S(1)}, f32[64,64]{1,0:T(8,128)S(1)}, f32[64,512]{1,0:T(8,128)S(1)}, f32[2,64,32]{2,1,0:T(8,128)S(1)}) custom-call(bf16[2,64,8192]{2,1,0:T(8,128)(2,1)} %bitcast.13, f32[2,64,8192]{2,1,0:T(8,128)} %bitcast.12, f32[64,512]{1,0:T(8,128)} %bitcast.14), custom_call_target="tpu_custom_call" | custom-call | tf_op jit(solution)/shard_map/pallas_call | solution.py:470
  70.9 4.6 %shard_map.59 = (f32[2,64,8192]{2,1,0:T(8,128)}, f32[64,64]{1,0:T(8,128)}, f32[64,512]{1,0:T(8,128)}) custom-call(f32[2,64,8192]{2,1,0:T(8,128)S(1)} %get-tuple-element.11.merged, f32[64,8192]{1,0:T(8,128)S(1)} %get-tuple-element.12.total, f32[2,64,32]{2,1,0:T(8,128)S(1)} %get-tuple-element.13.folded, f32[64,64]{1,0:T(8,128)S(1)} %get-tuple-element.14.left_in, ...), custom_call_target="tpu_custom_call" | custom-call | tf_op jit(solution)/shard_map/pallas_call | solution.py:506

commit v8 on v6

--- a/solution.py
+++ b/solution.py
@@ -41,8 +41,7 @@
     plane_first = [core, near + across, far]
     far_first = [core, far, near + across]
     reduce_parts = [
-        (0, 16, plane_first), (16, 32, plane_first), (32, 40, plane_first),
-        (40, 48, far_first), (48, 64, far_first),
+        (0, 32, plane_first), (32, 40, plane_first), (40, 64, far_first),
     ]
     plane = near + across if share else near
     gather_parts = [(0, 40, [far, plane, core]), (40, 64, [plane, far, core])]

time: 65.6 us -> 66.2 us (level)
  no operation moved by 1% of the time
where the time goes in v8:
time: 66.2 us; the launch traced here: 66 us
  Pallas kernels  65.4 us (99%)
    pallas_call x1, Pallas kernels, shards(): pl.pallas_call(functools.partial(exchange, n, replicas, share), out_shape...  60.8 us
    pallas_call x1, Pallas kernels, shards(): pl.pallas_call(finish, grid=(cols // block,), out_shape=[jax.ShapeDtypeSt...  4.59 us

profile of v8, /device:TPU:0, one launch (start us, length us, event | category | flops | bytes accessed | tf_op | source)
XLA Modules:
  0.0 66.0 jit_solution(14968255863242713293)
XLA Ops:
  0.6 60.8 %shard_map.58 = (f32[2,64,8192]{2,1,0:T(8,128)S(1)}, f32[64,8192]{1,0:T(8,128)S(1)}, f32[64,64]{1,0:T(8,128)S(1)}, f32[64,512]{1,0:T(8,128)S(1)}, f32[2,64,32]{2,1,0:T(8,128)S(1)}) custom-call(bf16[2,64,8192]{2,1,0:T(8,128)(2,1)} %bitcast.13, f32[2,64,8192]{2,1,0:T(8,128)} %bitcast.12, f32[64,512]{1,0:T(8,128)} %bitcast.14), custom_call_target="tpu_custom_call" | custom-call | tf_op jit(solution)/shard_map/pallas_call | solution.py:465
  61.4 4.6 %shard_map.59 = (f32[2,64,8192]{2,1,0:T(8,128)}, f32[64,64]{1,0:T(8,128)}, f32[64,512]{1,0:T(8,128)}) custom-call(f32[2,64,8192]{2,1,0:T(8,128)S(1)} %get-tuple-element.11.merged, f32[64,8192]{1,0:T(8,128)S(1)} %get-tuple-element.12.total, f32[2,64,32]{2,1,0:T(8,128)S(1)} %get-tuple-element.13.folded, f32[64,64]{1,0:T(8,128)S(1)} %get-tuple-element.14.left_in, ...), custom_call_target="tpu_custom_call" | custom-call | tf_op jit(solution)/shard_map/pallas_call | solution.py:501

commit v9 on v8

--- a/solution.py
+++ b/solution.py
@@ -41,7 +41,7 @@
     plane_first = [core, near + across, far]
     far_first = [core, far, near + across]
     reduce_parts = [
-        (0, 32, plane_first), (32, 40, plane_first), (40, 64, far_first),
+        (0, 16, plane_first), (16, 32, plane_first), (32, 48, plane_first), (48, 64, far_first),
     ]
     plane = near + across if share else near
     gather_parts = [(0, 40, [far, plane, core]), (40, 64, [plane, far, core])]
@@ -496,7 +496,7 @@
             ),
         )(grads, errors, basis_t)
 
-        block = 1024
+        block = 2048
         whole = lambda a: pl.BlockSpec(a.shape, lambda i: (0,) * a.ndim)
         new_errors, left_t, own_basis = pl.pallas_call(
             finish,

time: 66.2 us -> 62.6 us (0.946)
  Pallas kernels: 65.4 us -> 61.8 us
    pallas_call x1, Pallas kernels: 60.8 us -> 58.7 us  [shards(): pl.pallas_call(functools.partial(exchange, n, replicas, share), out_shape...]
    pallas_call x1, Pallas kernels: 4.59 us -> 3.08 us  [shards(): pl.pallas_call(finish, grid=(cols // block,), out_shape=[jax.ShapeDtypeSt...]
where the time goes in v9:
time: 62.6 us; the launch traced here: 62.4 us
  Pallas kernels  61.8 us (99%)
  between operations  0.64 us (1%)
    pallas_call x1, Pallas kernels, shards(): pl.pallas_call(functools.partial(exchange, n, replicas, share), out_shape...  58.7 us
    pallas_call x1, Pallas kernels, shards(): pl.pallas_call(finish, grid=(cols // block,), out_shape=[jax.ShapeDtypeSt...  3.08 us

profile of v9, /device:TPU:0, one launch (start us, length us, event | category | flops | bytes accessed | tf_op | source)
XLA Modules:
  0.0 62.4 jit_solution(11872921042285017690)
XLA Ops:
  0.6 58.7 %shard_map.58 = (f32[2,64,8192]{2,1,0:T(8,128)S(1)}, f32[64,8192]{1,0:T(8,128)S(1)}, f32[64,64]{1,0:T(8,128)S(1)}, f32[64,512]{1,0:T(8,128)S(1)}, f32[2,64,32]{2,1,0:T(8,128)S(1)}) custom-call(bf16[2,64,8192]{2,1,0:T(8,128)(2,1)} %bitcast.13, f32[2,64,8192]{2,1,0:T(8,128)} %bitcast.12, f32[64,512]{1,0:T(8,128)} %bitcast.14), custom_call_target="tpu_custom_call" | custom-call | tf_op jit(solution)/shard_map/pallas_call | solution.py:465
  59.4 3.1 %shard_map.59 = (f32[2,64,8192]{2,1,0:T(8,128)}, f32[64,64]{1,0:T(8,128)}, f32[64,512]{1,0:T(8,128)}) custom-call(f32[2,64,8192]{2,1,0:T(8,128)S(1)} %get-tuple-element.11.merged, f32[64,8192]{1,0:T(8,128)S(1)} %get-tuple-element.12.total, f32[2,64,32]{2,1,0:T(8,128)S(1)} %get-tuple-element.13.folded, f32[64,64]{1,0:T(8,128)S(1)} %get-tuple-element.14.left_in, ...), custom_call_target="tpu_custom_call" | custom-call | tf_op jit(solution)/shard_map/pallas_call | solution.py:501
